TPU v7x, 32 devices: a whole 2x2x4 slice. The times are simulated.
32 devices in a mesh: dp: 16 (over z, x, core), section: 2 (over y).
Axes of the slice: x: 2, y: 2, z: 4, core: 2. Of those that a mesh axis runs over, the one named last changes fastest.
Arguments:
- features: bfloat16 [32, 16, 5120], P('dp'), may hold values from -6 to 6
- target: bfloat16 [32, 16, 5120], P('dp'), may hold values from -6 to 6
- timesteps: int32 [32], P('dp'), may hold values from 0 to 999
- conv_one: bfloat16 [2, 2880, 320], P('section'), may hold values from -0.109375 to 0.109375
- conv_two: bfloat16 [2, 2880, 320], P('section'), may hold values from -0.109375 to 0.109375
- time_proj: float32 [2, 320, 320], P('section'), may hold values from -0.3125 to 0.3125
Outputs:
- grad_one: float32 [2, 2880, 320], P('section')
- grad_two: float32 [2, 2880, 320], P('section')
- grad_time: float32 [2, 320, 320], P('section')
All inputs are finite; a program needn't handle non-finite values.
Results may differ from a plain program's by a relative error of at most 0.002.
Values sent between devices are 32-bit elements; how exact they have to be, the bound alone decides.
A program may use at most 128 MiB of HBM per device.

v0:
```python
import math

import jax
import jax.numpy as jnp
from jax import lax
from jax.sharding import PartitionSpec as P

CH = 320
TE = 320
GROUPS = 32
HEIGHT = 16
WIDTH = 16
MICRO = 2


def from_partner(value, axis, apart):
    mask = 2**apart
    pairs = [(source, source ^ mask) for source in range(lax.axis_size(axis))]
    return lax.ppermute(value, axis, pairs)


def passed_along(block, axis, distance):
    devices = range(lax.axis_size(axis))
    route = [(i - distance, i) for i in devices if i - distance in devices]
    return lax.ppermute(block, axis, route)


def embed_times(times):
    middle = TE // 2
    freqs = jnp.exp(-math.log(10000.0) * jnp.arange(middle, dtype=jnp.float32) / middle)
    angles = times.astype(jnp.float32)[:, None] * freqs[None, :]
    return jnp.concatenate([jnp.cos(angles), jnp.sin(angles)], axis=1)


def norm_silu(values):
    count, height, width, chans = values.shape
    grouped = values.reshape(count, height, width, GROUPS, chans // GROUPS)
    center = jnp.mean(grouped, axis=(1, 2, 4), keepdims=True)
    spread = jnp.mean(jnp.square(grouped - center), axis=(1, 2, 4), keepdims=True)
    normed = ((grouped - center) * lax.rsqrt(spread + 1e-05)).reshape(values.shape)
    return jax.nn.silu(normed)


def patches(acts):
    height, width = (acts.shape[1], acts.shape[2])
    padded = jnp.pad(acts, ((0, 0), (1, 1), (1, 1), (0, 0)))
    taps = [
        padded[:, row_shift : row_shift + height, col_shift : col_shift + width, :]
        for row_shift in range(3)
        for col_shift in range(3)
    ]
    return jnp.concatenate(taps, axis=-1)


def conv_apply(acts, weights):
    cols = patches(acts)
    flat = cols.reshape(-1, cols.shape[-1])
    result = jnp.dot(flat, weights, preferred_element_type=jnp.float32)
    return result.reshape(acts.shape[:3] + (weights.shape[1],))


def conv_back(grads, weights):
    count, height, width, chans = grads.shape
    flat = grads.reshape(-1, chans)
    spread_back = jnp.dot(flat, weights.T, preferred_element_type=jnp.float32)
    in_chans = weights.shape[0] // 9
    spread_back = spread_back.reshape(count, height, width, 9, in_chans)
    padded = jnp.zeros((count, height + 2, width + 2, in_chans), jnp.float32)
    for index in range(9):
        row_shift, col_shift = (index // 3, index % 3)
        padded = padded.at[:, row_shift : row_shift + height, col_shift : col_shift + width, :].add(
            spread_back[:, :, :, index, :]
        )
    return padded[:, 1:-1, 1:-1, :]


def weight_grad(acts, grads):
    cols = patches(acts)
    flat = cols.reshape(-1, cols.shape[-1])
    return lax.dot_general(
        flat,
        grads.reshape(-1, grads.shape[-1]),
        (((0,), (0,)), ((), ())),
        preferred_element_type=jnp.float32,
    )


def section_forward(section_in, bias_rows, weight_one, weight_two):
    acts_one = norm_silu(section_in).astype(jnp.bfloat16)
    conv_mid = conv_apply(acts_one, weight_one) + bias_rows[:, None, None, :]
    acts_two = norm_silu(conv_mid).astype(jnp.bfloat16)
    return section_in + conv_apply(acts_two, weight_two)


def section_backward(section_in, bias_rows, weight_one, weight_two, grad_out):
    acts_one = norm_silu(section_in).astype(jnp.bfloat16)
    conv_mid = conv_apply(acts_one, weight_one) + bias_rows[:, None, None, :]
    acts_two = norm_silu(conv_mid).astype(jnp.bfloat16)
    grad_low = grad_out.astype(jnp.bfloat16)
    delta_two = weight_grad(acts_two, grad_low)
    grad_acts_two = conv_back(grad_low, weight_two)
    grad_mid = jax.vjp(norm_silu, conv_mid)[1](grad_acts_two)[0]
    grad_bias = jnp.sum(grad_mid, axis=(1, 2))
    grad_mid_low = grad_mid.astype(jnp.bfloat16)
    delta_one = weight_grad(acts_one, grad_mid_low)
    grad_acts_one = conv_back(grad_mid_low, weight_one)
    grad_in = grad_out + jax.vjp(norm_silu, section_in)[1](grad_acts_one)[0]
    return (grad_in, delta_one, delta_two, grad_bias)


def pick_slot(buffer, slot):
    return lax.dynamic_index_in_dim(buffer, slot, 0, keepdims=False)


def put_slot(buffer, slot, value, enabled):
    fresh = jnp.where(enabled, value, pick_slot(buffer, slot))
    return lax.dynamic_update_index_in_dim(buffer, fresh, slot, 0)


def local(features, target, timesteps, conv_one, conv_two, time_proj):
    sections = lax.axis_size("section")
    section_pos = lax.axis_index("section")
    middle = sections // 2
    partner = sections - 1 - section_pos
    is_decoder = section_pos >= middle
    is_encoder = section_pos < middle
    is_first = section_pos == 0
    is_last = section_pos == sections - 1
    images = features.shape[0] // MICRO
    row_len = WIDTH * CH
    weight_one = conv_one[0]
    weight_two = conv_two[0]
    embedded = embed_times(timesteps)
    bias_all = jnp.dot(embedded, time_proj[0], precision=lax.Precision.HIGHEST)
    feats_micro = features.reshape(MICRO, images, HEIGHT, row_len)
    target_micro = target.reshape(MICRO, images, HEIGHT, row_len)
    bias_micro = bias_all.reshape(MICRO, images, CH)
    embed_micro = embedded.reshape(MICRO, images, TE)
    tick_count = MICRO + sections - 1
    bit_count = sections.bit_length() - 1
    bit_list = list(range(bit_count))
    image_shape = (images, HEIGHT, WIDTH, CH)
    flat_shape = (images, HEIGHT, row_len)
    stack_shape = (middle,) + flat_shape
    scale = 1.0 / math.sqrt(HEIGHT * WIDTH)

    def route_forward(sent):
        moved = sent
        for bit in bit_list:
            moved = from_partner(moved, "section", bit)
        return moved

    def route_backward(sent):
        moved = sent
        for bit in bit_list:
            moved = from_partner(moved, "section", bit)
        return moved

    def forward_tick(carry, tick):
        incoming, skip_buffer, skip_stack, saved_inputs, last_outputs = carry
        micro_now = tick - section_pos
        active = (micro_now >= 0) & (micro_now < MICRO)
        slot = jnp.clip(micro_now, 0, MICRO - 1)
        given = jnp.where(is_first, pick_slot(feats_micro, slot).astype(jnp.float32), incoming)
        skip_now = pick_slot(skip_buffer, slot)
        skip_part = jnp.where(is_decoder, skip_now, 0.0)
        section_in = (given + skip_part).reshape(image_shape)
        bias_rows = pick_slot(bias_micro, slot)
        result = lax.cond(
            active,
            lambda: section_forward(section_in, bias_rows, weight_one, weight_two),
            lambda: jnp.zeros(image_shape, jnp.float32),
        )
        result = result.reshape(flat_shape)
        saved_inputs = put_slot(saved_inputs, slot, section_in, active)
        last_outputs = put_slot(last_outputs, slot, result, active & is_last)
        incoming = passed_along(result, "section", 1)
        arrived = route_forward(result)
        skip_micro = tick - partner
        usable = is_decoder & (skip_micro >= 0) & (skip_micro < MICRO)
        skip_slot = jnp.clip(skip_micro, 0, MICRO - 1)
        skip_buffer = put_slot(skip_buffer, skip_slot, arrived, usable)
        return ((incoming, skip_buffer, skip_stack, saved_inputs, last_outputs), None)

    start_fwd = (
        jnp.zeros(flat_shape, jnp.float32),
        jnp.zeros((MICRO,) + flat_shape, jnp.float32),
        jnp.zeros(stack_shape, jnp.float32),
        jnp.zeros((MICRO,) + image_shape, jnp.float32),
        jnp.zeros((MICRO,) + flat_shape, jnp.float32),
    )
    fwd_done, unused_out = lax.scan(forward_tick, start_fwd, jnp.arange(tick_count))
    saved_inputs, last_outputs = (fwd_done[3], fwd_done[4])

    def backward_tick(carry, tick):
        incoming, skip_grads, grad_stack, total_one, total_two, total_time = carry
        micro_now = tick - (sections - 1 - section_pos)
        active = (micro_now >= 0) & (micro_now < MICRO)
        slot = jnp.clip(micro_now, 0, MICRO - 1)
        loss_grad = (
            pick_slot(last_outputs, slot) - pick_slot(target_micro, slot).astype(jnp.float32)
        ) * scale
        given = jnp.where(is_last, loss_grad, incoming)
        skip_now = pick_slot(skip_grads, slot)
        given = given + jnp.where(is_encoder, skip_now, 0.0)
        grad_out = given.reshape(image_shape)
        section_in = pick_slot(saved_inputs, slot)
        bias_rows = pick_slot(bias_micro, slot)

        def run_section():
            return section_backward(section_in, bias_rows, weight_one, weight_two, grad_out)

        def quiet_section():
            return (
                jnp.zeros(image_shape, jnp.float32),
                jnp.zeros(weight_one.shape, jnp.float32),
                jnp.zeros(weight_two.shape, jnp.float32),
                jnp.zeros((images, CH), jnp.float32),
            )

        grad_in, delta_one, delta_two, grad_bias = lax.cond(active, run_section, quiet_section)
        delta_time = jnp.dot(
            pick_slot(embed_micro, slot).T, grad_bias, precision=lax.Precision.HIGHEST
        )
        grad_flat = grad_in.reshape(flat_shape)
        incoming = passed_along(grad_flat, "section", -1)
        arrived = route_backward(grad_flat)
        skip_micro = tick - section_pos
        usable = is_encoder & (skip_micro >= 0) & (skip_micro < MICRO)
        skip_slot = jnp.clip(skip_micro, 0, MICRO - 1)
        skip_grads = put_slot(skip_grads, skip_slot, arrived, usable)
        return (
            (
                incoming,
                skip_grads,
                grad_stack,
                total_one + delta_one,
                total_two + delta_two,
                total_time + delta_time,
            ),
            None,
        )

    start_bwd = (
        jnp.zeros(flat_shape, jnp.float32),
        jnp.zeros((MICRO,) + flat_shape, jnp.float32),
        jnp.zeros(stack_shape, jnp.float32),
        jnp.zeros(weight_one.shape, jnp.float32),
        jnp.zeros(weight_two.shape, jnp.float32),
        jnp.zeros((TE, CH), jnp.float32),
    )
    finished, unused_back = lax.scan(backward_tick, start_bwd, jnp.arange(tick_count))
    total_one, total_two, total_time = (finished[3], finished[4], finished[5])
    sum_one, sum_two, sum_time = lax.psum((total_one, total_two, total_time), "dp")
    return (sum_one[None], sum_two[None], sum_time[None])


def solution(mesh):
    placed = (
        P("dp", None, None),
        P("dp", None, None),
        P("dp"),
        P("section", None, None),
        P("section", None, None),
        P("section", None, None),
    )
    return jax.shard_map(
        local,
        mesh=mesh,
        in_specs=placed,
        out_specs=(P("section", None, None), P("section", None, None), P("section", None, None)),
        check_vma=False,
    )
```

profile of v0, /device:TPU:1, one launch (start us, length us, event | category | flops | bytes accessed | tf_op | source)
XLA Modules:
  0.0 740.7 jit_solution(14458762282777624528)
XLA Ops:
  18.5 158.4 %while.54 = (s32[]{:T(128)}, f32[1,16,5120]{2,1,0:T(8,128)}, f32[2,1,16,5120]{3,2,1,0:T(8,128)}, f32[2,1,16,16,320]{4,3,2,1,0:T(8,128)S(1)}, f32[2,1,16,5120]{3,...) while((s32[]{:T(128)}, f32[1,16,5120]{2,1,0:T(8,128)}, ...), condition=%wide.region_11.12_spmd, body=%wide.region_0.11_spmd.sunk | while | flops 946831424 | bytes 29991520 | solution.py:192
  20.8 35.2 %conditional.5 = (f32[1,16,5120]{2,1,0:T(8,128)}, f32[1,1,16,5120]{3,2,1,0:T(8,128)}) conditional(s32[]{:T(128)} %convert_element_type.150, () %tuple.224, (f32[1,16,5120]{2,1,0:T(8,128)S(1)}, bf16[2880,320]{0,1:T(8,128)(2,1)}, f32[2,1,320]{2,1,0:T(1,128)S(1)}, s32[]{:T(128)}, bf16[2880,320]{0,1:T(8,128)(2,1)}) %tuple.225), branch_computations={%region_1.1_spmd, %region_2.10_spmd} | conditional | flops 946257984 | bytes 21831336 | solution.py:169
  72.9 35.2 %conditional.5 = (f32[1,16,5120]{2,1,0:T(8,128)}, f32[1,1,16,5120]{3,2,1,0:T(8,128)}) conditional(s32[]{:T(128)} %convert_element_type.150, () %tuple.224, (f32[1,16,5120]{2,1,0:T(8,128)S(1)}, bf16[2880,320]{0,1:T(8,128)(2,1)}, f32[2,1,320]{2,1,0:T(1,128)S(1)}, s32[]{:T(128)}, bf16[2880,320]{0,1:T(8,128)(2,1)}) %tuple.225), branch_computations={%region_1.1_spmd, %region_2.10_spmd} | conditional | flops 946257984 | bytes 21831336 | solution.py:169
  120.0 4.2 collective-permute-done
  128.0 36.0 %collective-permute-start.1 = (f32[1,16,5120]{2,1,0:T(8,128)}, f32[1,16,5120]{2,1,0:T(8,128)}, u32[]{:S(2)}, u32[]{:S(2)}) collective-permute-start(f32[1,16,5120]{2,1,0:T(8,128)} %get-tuple-element.1093), channel_id=1, source_target_pairs={{0,1},{1,0},{2,3},{3,2},{4,5},{5,4},{6,7},{7,6},{8,9},{9,8},{10,11... | collective-permute-start | bytes 983048 | tf_op jit(solution)/shard_map/while/body/eval_jaxpr/ppermute | solution.py:19
  172.6 4.3 collective-permute-done
  178.5 377.7 %while.55 = (s32[]{:T(128)}, f32[1,16,5120]{2,1,0:T(8,128)}, f32[2,1,16,5120]{3,2,1,0:T(8,128)}, f32[2880,320]{0,1:T(8,128)}, f32[2880,320]{0,1:T(8,128)}, /*ind...) while((s32[]{:T(128)}, f32[1,16,5120]{2,1,0:T(8,128)}, ...), condition=%wide.region_37.38_spmd.clone, body=%wide.region_12.37_spmd.clone.sunk | while | flops 2371809792 | bytes 146409552 | solution.py:252
  179.9 5.1 conditional.6
  185.1 106.5 %collective-permute-start.3 = (f32[1,16,5120]{2,1,0:T(8,128)}, f32[1,16,5120]{2,1,0:T(8,128)}, u32[]{:S(2)}, u32[]{:S(2)}) collective-permute-start(f32[1,16,5120]{2,1,0:T(8,128)} %get-tuple-element.1115), channel_id=1, source_target_pairs={{0,1},{1,0},{2,3},{3,2},{4,5},{5,4},{6,7},{7,6},{8,9},{9,8},{10,11... | collective-permute-start | bytes 983048 | tf_op jit(solution)/shard_map/while/body/eval_jaxpr/ppermute | solution.py:19
  293.5 7.2 select_add_fusion.5
  305.9 109.5 %conditional.6 = (f32[2880,320]{0,1:T(8,128)}, f32[2880,320]{0,1:T(8,128)}, f32[1,16,5120]{2,1,0:T(8,128)}, f32[320]{0:T(512)S(1)}) conditional(s32[]{:T(128)} %convert_element_type.151, () %tuple.228, (f32[2,1,16,16,320]{4,3,2,1,0:T(8,128)S(1)}, s32[]{:T(128)}, pred[]{:T(512)}, f32[2,1,16,5120]{3,2,1,0:T(8,128)}, ...), branch_computations={%region_13.13_spmd, %region_14.36_spmd} | conditional | flops 2367734272 | bytes 101839344 | solution.py:221
  311.7 5.4 scatter-add.14
  321.4 5.4 scatter-add.15
  365.7 5.4 scatter-add.46
  374.0 5.4 scatter-add.49
  418.1 9.4 %select_add_fusion.5 = (f32[2880,320]{0,1:T(8,128)}, f32[2880,320]{0,1:T(8,128)}) fusion(f32[2880,320]{0,1:T(8,128)} %get-tuple-element.1116, f32[2880,320]{0,1:T(8,128)} %get-tuple-element.1212, pred[]{:T(512)S(6)} %compare.109, f32[2880,320]{0,1:T(8,128)} %get-tuple-element.1117, f32[2880,320]{0,1:T(8,128)} %get-tuple-element.1211), kind=kLoop, calls=%fused_computation.172.clone.1 | loop fusion | flops 3686400 | bytes 22118400 | tf_op jit(solution)/shard_map/while/body/eval_jaxpr/add | solution.py:238
  432.6 109.5 %conditional.6 = (f32[2880,320]{0,1:T(8,128)}, f32[2880,320]{0,1:T(8,128)}, f32[1,16,5120]{2,1,0:T(8,128)}, f32[320]{0:T(512)S(1)}) conditional(s32[]{:T(128)} %convert_element_type.151, () %tuple.228, (f32[2,1,16,16,320]{4,3,2,1,0:T(8,128)S(1)}, s32[]{:T(128)}, pred[]{:T(512)}, f32[2,1,16,5120]{3,2,1,0:T(8,128)}, ...), branch_computations={%region_13.13_spmd, %region_14.36_spmd} | conditional | flops 2367734272 | bytes 101839344 | solution.py:221
  438.4 5.4 scatter-add.14
  448.0 5.4 scatter-add.15
  492.4 5.4 scatter-add.46
  500.7 5.4 scatter-add.49
  544.1 9.4 %select_add_fusion.5 = (f32[2880,320]{0,1:T(8,128)}, f32[2880,320]{0,1:T(8,128)}) fusion(f32[2880,320]{0,1:T(8,128)} %get-tuple-element.1116, f32[2880,320]{0,1:T(8,128)} %get-tuple-element.1212, pred[]{:T(512)S(6)} %compare.109, f32[2880,320]{0,1:T(8,128)} %get-tuple-element.1117, f32[2880,320]{0,1:T(8,128)} %get-tuple-element.1211), kind=kLoop, calls=%fused_computation.172.clone.1 | loop fusion | flops 3686400 | bytes 22118400 | tf_op jit(solution)/shard_map/while/body/eval_jaxpr/add | solution.py:238
  556.2 170.6 %all-reduce.9.cloned.1.call-done = (f32[1,2880,320]{1,2,0:T(8,128)}, f32[1,2880,320]{1,2,0:T(8,128)}, f32[1,320,320]{2,1,0:T(8,128)}) async-done(((f32[1,2880,320]{1,2,0:T(8,128)}, f32[1,2880,320]{1,2,0:T(8,128)}, f32[1,320,320]{2,1,0:T(8,128)}), (f32[1,2880,320]{1,2,0:T(8,128)}, f32[1,2880,320]{1,2,0:T(8,128)}, f32[1,320,320]{2,1,0:T(8,128)})) %all-reduce.9.cloned.1.call-update) | async-done | bytes 7782416 | tf_op jit(solution)/shard_map/psum | solution.py:254
  726.9 4.3 copy.122
  (424 shorter events, 323.9 us)
Async XLA Ops:
  7.2 719.7 %all-reduce.9.cloned.1.call-start = ((), (), s32[]{:S(2)}) async-start(), calls=%async_computation | async-start | bytes 16056320 | tf_op jit(solution)/shard_map/psum | solution.py:254
  56.0 9.6 %collective-permute-start.1 = (f32[1,16,5120]{2,1,0:T(8,128)}, f32[1,16,5120]{2,1,0:T(8,128)}, u32[]{:S(2)}, u32[]{:S(2)}) collective-permute-start(f32[1,16,5120]{2,1,0:T(8,128)} %get-tuple-element.1093), channel_id=1, source_target_pairs={{0,1},{1,0},{2,3},{3,2},{4,5},{5,4},{6,7},{7,6},{8,9},{9,8},{10,11... | collective-permute-start | bytes 983048 | tf_op jit(solution)/shard_map/while/body/eval_jaxpr/ppermute | solution.py:19
  56.0 14.6 %collective-permute-start = (f32[1,16,5120]{2,1,0:T(8,128)}, f32[1,16,5120]{2,1,0:T(8,128)}, u32[]{:S(2)}, u32[]{:S(2)}) collective-permute-start(f32[1,16,5120]{2,1,0:T(8,128)} %get-tuple-element.1093), channel_id=1, source_target_pairs={{0,1},{2,3},{4,5},{6,7},{8,9},{10,11},{12,13},{14,15},{16,17},{18,... | collective-permute-start | bytes 983048 | tf_op jit(solution)/shard_map/while/body/eval_jaxpr/ppermute | solution.py:25
  108.2 10.1 %collective-permute-start.1 = (f32[1,16,5120]{2,1,0:T(8,128)}, f32[1,16,5120]{2,1,0:T(8,128)}, u32[]{:S(2)}, u32[]{:S(2)}) collective-permute-start(f32[1,16,5120]{2,1,0:T(8,128)} %get-tuple-element.1093), channel_id=1, source_target_pairs={{0,1},{1,0},{2,3},{3,2},{4,5},{5,4},{6,7},{7,6},{8,9},{9,8},{10,11... | collective-permute-start | bytes 983048 | tf_op jit(solution)/shard_map/while/body/eval_jaxpr/ppermute | solution.py:19
  110.5 13.8 %collective-permute-start = (f32[1,16,5120]{2,1,0:T(8,128)}, f32[1,16,5120]{2,1,0:T(8,128)}, u32[]{:S(2)}, u32[]{:S(2)}) collective-permute-start(f32[1,16,5120]{2,1,0:T(8,128)} %get-tuple-element.1093), channel_id=1, source_target_pairs={{0,1},{2,3},{4,5},{6,7},{8,9},{10,11},{12,13},{14,15},{16,17},{18,... | collective-permute-start | bytes 983048 | tf_op jit(solution)/shard_map/while/body/eval_jaxpr/ppermute | solution.py:25
  128.0 42.9 %collective-permute-start.1 = (f32[1,16,5120]{2,1,0:T(8,128)}, f32[1,16,5120]{2,1,0:T(8,128)}, u32[]{:S(2)}, u32[]{:S(2)}) collective-permute-start(f32[1,16,5120]{2,1,0:T(8,128)} %get-tuple-element.1093), channel_id=1, source_target_pairs={{0,1},{1,0},{2,3},{3,2},{4,5},{5,4},{6,7},{7,6},{8,9},{9,8},{10,11... | collective-permute-start | bytes 983048 | tf_op jit(solution)/shard_map/while/body/eval_jaxpr/ppermute | solution.py:19
  164.1 12.8 %collective-permute-start = (f32[1,16,5120]{2,1,0:T(8,128)}, f32[1,16,5120]{2,1,0:T(8,128)}, u32[]{:S(2)}, u32[]{:S(2)}) collective-permute-start(f32[1,16,5120]{2,1,0:T(8,128)} %get-tuple-element.1093), channel_id=1, source_target_pairs={{0,1},{2,3},{4,5},{6,7},{8,9},{10,11},{12,13},{14,15},{16,17},{18,... | collective-permute-start | bytes 983048 | tf_op jit(solution)/shard_map/while/body/eval_jaxpr/ppermute | solution.py:25
  185.1 116.7 %collective-permute-start.3 = (f32[1,16,5120]{2,1,0:T(8,128)}, f32[1,16,5120]{2,1,0:T(8,128)}, u32[]{:S(2)}, u32[]{:S(2)}) collective-permute-start(f32[1,16,5120]{2,1,0:T(8,128)} %get-tuple-element.1115), channel_id=1, source_target_pairs={{0,1},{1,0},{2,3},{3,2},{4,5},{5,4},{6,7},{7,6},{8,9},{9,8},{10,11... | collective-permute-start | bytes 983048 | tf_op jit(solution)/shard_map/while/body/eval_jaxpr/ppermute | solution.py:19
  291.6 12.9 %collective-permute-start.2 = (f32[1,16,5120]{2,1,0:T(8,128)}, f32[1,16,5120]{2,1,0:T(8,128)}, u32[]{:S(2)}, u32[]{:S(2)}) collective-permute-start(f32[1,16,5120]{2,1,0:T(8,128)} %get-tuple-element.1115), channel_id=1, source_target_pairs={{1,0},{3,2},{5,4},{7,6},{9,8},{11,10},{13,12},{15,14},{17,16},{19,... | collective-permute-start | bytes 983048 | tf_op jit(solution)/shard_map/while/body/eval_jaxpr/ppermute | solution.py:25
  293.5 7.2 copy-start.7
  293.5 11.0 %copy-start.5 = (bf16[2880,320]{1,0:T(8,128)(2,1)S(1)}, bf16[2880,320]{1,0:T(8,128)(2,1)}, u32[]{:S(2)}) copy-start(bf16[2880,320]{1,0:T(8,128)(2,1)} %copy-done.4) | copy-start | bytes 5529604 | tf_op jit(solution)/shard_map/while
  308.1 9.6 %copy-start.13 = (s32[4]{0:T(128)S(1)}, s32[4]{0:T(128)}, u32[]{:S(2)}) copy-start(s32[4]{0:T(128)} %constant.652.clone) | copy-start | bytes 52 | tf_op jit(solution)/shard_map/while/body/eval_jaxpr/cond
  390.5 12.2 %copy-start.6 = (f32[1,16,5120]{2,1,0:T(8,128)S(1)}, f32[1,16,5120]{2,1,0:T(8,128)}, u32[]{:S(2)}) copy-start(f32[1,16,5120]{2,1,0:T(8,128)} %get-tuple-element.842) | copy-start | bytes 983044 | tf_op jit(solution)/shard_map/while/body/eval_jaxpr/cond
  415.4 14.0 %collective-permute-start.3 = (f32[1,16,5120]{2,1,0:T(8,128)}, f32[1,16,5120]{2,1,0:T(8,128)}, u32[]{:S(2)}, u32[]{:S(2)}) collective-permute-start(f32[1,16,5120]{2,1,0:T(8,128)} %get-tuple-element.1115), channel_id=1, source_target_pairs={{0,1},{1,0},{2,3},{3,2},{4,5},{5,4},{6,7},{7,6},{8,9},{9,8},{10,11... | collective-permute-start | bytes 983048 | tf_op jit(solution)/shard_map/while/body/eval_jaxpr/ppermute | solution.py:19
  416.1 15.1 %collective-permute-start.2 = (f32[1,16,5120]{2,1,0:T(8,128)}, f32[1,16,5120]{2,1,0:T(8,128)}, u32[]{:S(2)}, u32[]{:S(2)}) collective-permute-start(f32[1,16,5120]{2,1,0:T(8,128)} %get-tuple-element.1115), channel_id=1, source_target_pairs={{1,0},{3,2},{5,4},{7,6},{9,8},{11,10},{13,12},{15,14},{17,16},{19,... | collective-permute-start | bytes 983048 | tf_op jit(solution)/shard_map/while/body/eval_jaxpr/ppermute | solution.py:25
  418.1 9.4 %copy-start.7 = (f32[2,1,16,5120]{3,2,1,0:T(8,128)S(1)}, f32[2,1,16,5120]{3,2,1,0:T(8,128)}, u32[]{:S(2)}) copy-start(f32[2,1,16,5120]{3,2,1,0:T(8,128)} %get-tuple-element.1210) | copy-start | bytes 1966084 | tf_op jit(solution)/shard_map/while
  418.1 13.1 %copy-start.5 = (bf16[2880,320]{1,0:T(8,128)(2,1)S(1)}, bf16[2880,320]{1,0:T(8,128)(2,1)}, u32[]{:S(2)}) copy-start(bf16[2880,320]{1,0:T(8,128)(2,1)} %copy-done.4) | copy-start | bytes 5529604 | tf_op jit(solution)/shard_map/while
  434.8 9.6 %copy-start.13 = (s32[4]{0:T(128)S(1)}, s32[4]{0:T(128)}, u32[]{:S(2)}) copy-start(s32[4]{0:T(128)} %constant.652.clone) | copy-start | bytes 52 | tf_op jit(solution)/shard_map/while/body/eval_jaxpr/cond
  517.2 12.2 %copy-start.6 = (f32[1,16,5120]{2,1,0:T(8,128)S(1)}, f32[1,16,5120]{2,1,0:T(8,128)}, u32[]{:S(2)}) copy-start(f32[1,16,5120]{2,1,0:T(8,128)} %get-tuple-element.842) | copy-start | bytes 983044 | tf_op jit(solution)/shard_map/while/body/eval_jaxpr/cond
  542.1 13.3 %collective-permute-start.3 = (f32[1,16,5120]{2,1,0:T(8,128)}, f32[1,16,5120]{2,1,0:T(8,128)}, u32[]{:S(2)}, u32[]{:S(2)}) collective-permute-start(f32[1,16,5120]{2,1,0:T(8,128)} %get-tuple-element.1115), channel_id=1, source_target_pairs={{0,1},{1,0},{2,3},{3,2},{4,5},{5,4},{6,7},{7,6},{8,9},{9,8},{10,11... | collective-permute-start | bytes 983048 | tf_op jit(solution)/shard_map/while/body/eval_jaxpr/ppermute | solution.py:19
  542.1 14.1 %collective-permute-start.2 = (f32[1,16,5120]{2,1,0:T(8,128)}, f32[1,16,5120]{2,1,0:T(8,128)}, u32[]{:S(2)}, u32[]{:S(2)}) collective-permute-start(f32[1,16,5120]{2,1,0:T(8,128)} %get-tuple-element.1115), channel_id=1, source_target_pairs={{1,0},{3,2},{5,4},{7,6},{9,8},{11,10},{13,12},{15,14},{17,16},{19,... | collective-permute-start | bytes 983048 | tf_op jit(solution)/shard_map/while/body/eval_jaxpr/ppermute | solution.py:25
  544.1 9.4 %copy-start.7 = (f32[2,1,16,5120]{3,2,1,0:T(8,128)S(1)}, f32[2,1,16,5120]{3,2,1,0:T(8,128)}, u32[]{:S(2)}) copy-start(f32[2,1,16,5120]{3,2,1,0:T(8,128)} %get-tuple-element.1210) | copy-start | bytes 1966084 | tf_op jit(solution)/shard_map/while
  544.1 12.1 %copy-start.5 = (bf16[2880,320]{1,0:T(8,128)(2,1)S(1)}, bf16[2880,320]{1,0:T(8,128)(2,1)}, u32[]{:S(2)}) copy-start(bf16[2880,320]{1,0:T(8,128)(2,1)} %copy-done.4) | copy-start | bytes 5529604 | tf_op jit(solution)/shard_map/while
  726.9 7.0 copy-start.1
  (16 other events, 36.9 us)
Sparse Core Ops, SparseCore 0:
  556.4 170.4 all-reduce.8
where the time goes:
time: 746 us; the launch traced here: 741 us
  local copies, waits for them, and re-layouts  211 us (28%)
  waiting for transfers between devices  186 us (25%)
  starting transfers between devices  159 us (21%)
  other arithmetic  122 us (16%)
  matrix products  39.7 us (5%)
  between operations  14.1 us (2%)
  loops' own time  9.1 us (1%)
    psum x1, waiting for transfers between devices, local(): lax.psum((total_one, total_two, total_time), 'dp')  171 us
    ppermute x6, starting transfers between devices, from_partner(): return lax.ppermute(value, axis, pairs)  146 us
    scatter-add x28, local copies, waits for them, and re-layouts, conv_back(): padded.at[:, row_shift:row_shift + height, col_shift:col_shift + width, :]  105 us
    concatenate x14, local copies, waits for them, and re-layouts, patches(): return jnp.concatenate(taps, axis=-1)  36.9 us
    add x3, other arithmetic, backward_tick(): total_two + delta_two  25.9 us
    add x20, other arithmetic, conv_back(): padded.at[:, row_shift:row_shift + height, col_shift:col_shift + width, :]  22.4 us
    dot_general x6, matrix products, conv_apply(): result = jnp.dot(flat, weights, preferred_element_type=jnp.float32)  21 us
    dynamic_update_slice x12, other arithmetic, put_slot(): return lax.dynamic_update_index_in_dim(buffer, fresh, slot, 0)  17.6 us
  transfers between devices with their start and end apart: 13, of which 8 were waited for; matrix products, arithmetic and copies ran while one was open for 7% of the time, Pallas kernels for 0%

commit v1 on v0

--- a/solution.py
+++ b/solution.py
@@ -3,6 +3,8 @@
 import jax
 import jax.numpy as jnp
 from jax import lax
+from jax.experimental import pallas as pl
+from jax.experimental.pallas import tpu as pltpu
 from jax.sharding import PartitionSpec as P
 
 CH = 320
@@ -255,6 +257,241 @@
     return (sum_one[None], sum_two[None], sum_time[None])
 
 
+PIX = HEIGHT * WIDTH
+KR = 3 * CH
+MESH_IDS = pl.DeviceIdType.MESH
+VMEM_BYTES = 56 * 1024 * 1024
+
+
+def group_mean(cols, same_group):
+    wide = jnp.broadcast_to(cols, (8, CH))
+    total = jnp.dot(
+        wide, same_group, precision=lax.Precision.HIGHEST, preferred_element_type=jnp.float32
+    )
+    return total[0:1, :] * (1.0 / (PIX * (CH // GROUPS)))
+
+
+def col_sum(values):
+    return jnp.sum(values, axis=0, keepdims=True)
+
+
+def norm_parts(values, same_group):
+    centered = values - group_mean(col_sum(values), same_group)
+    inv = lax.rsqrt(group_mean(col_sum(centered * centered), same_group) + 1e-05)
+    normed = centered * inv
+    gate = 1.0 / (1.0 + jnp.exp(-normed))
+    return normed, gate, inv
+
+
+def norm_back(parts, cotangent, same_group):
+    normed, gate, inv = parts
+    dn = cotangent * (gate * (1.0 + normed * (1.0 - gate)))
+    mean_dn = group_mean(col_sum(dn), same_group)
+    mean_dnn = group_mean(col_sum(dn * normed), same_group)
+    return inv * (dn - mean_dn - normed * mean_dnn)
+
+
+def side_taps(values):
+    column = lax.broadcasted_iota(jnp.int32, (PIX, CH), 0) % WIDTH
+    before = jnp.where(column == 0, 0.0, pltpu.roll(values, 1, 0))
+    after = jnp.where(column == WIDTH - 1, 0.0, pltpu.roll(values, PIX - 1, 0))
+    return before, values, after
+
+
+def stack_taps(parts):
+    return jnp.concatenate(parts, axis=1).astype(jnp.bfloat16)
+
+
+def add_rows(low, mid, high):
+    edge = jnp.zeros((WIDTH, CH), jnp.float32)
+    down = jnp.concatenate([edge, low[: PIX - WIDTH]], axis=0)
+    up = jnp.concatenate([high[WIDTH:], edge], axis=0)
+    return down + mid + up
+
+
+def images_of(rows):
+    return [rows[i * PIX : (i + 1) * PIX] for i in range(rows.shape[0] // PIX)]
+
+
+def conv_rows(taps, w_ref):
+    parts = [
+        jnp.dot(taps, w_ref[r * KR : (r + 1) * KR, :], preferred_element_type=jnp.float32)
+        for r in range(3)
+    ]
+    split = [images_of(part) for part in parts]
+    return [add_rows(*trio) for trio in zip(*split)]
+
+
+def conv_rows_back(low_rows, w_ref):
+    before, same, after = [
+        jnp.concatenate(part, axis=0).astype(jnp.bfloat16)
+        for part in zip(*[side_taps(rows) for rows in low_rows])
+    ]
+    sums = []
+    for r in range(3):
+        total = None
+        for c, side in enumerate((after, same, before)):
+            tap = (3 * r + c) * CH
+            part = lax.dot_general(
+                side, w_ref[tap : tap + CH, :], (((1,), (1,)), ((), ())),
+                preferred_element_type=jnp.float32,
+            )
+            total = part if total is None else total + part
+        sums.append(images_of(total))
+    return [add_rows(up, mid, down) for down, mid, up in zip(*sums)]
+
+
+def weight_rows(taps, low_rows, buf_ref, lane):
+    edge = jnp.zeros((WIDTH, CH), jnp.float32)
+    flipped = taps.T
+    for r in range(3):
+        moved = []
+        for rows in low_rows:
+            if r == 0:
+                moved.append(jnp.concatenate([rows[WIDTH:], edge], axis=0))
+            elif r == 1:
+                moved.append(rows)
+            else:
+                moved.append(jnp.concatenate([edge, rows[: PIX - WIDTH]], axis=0))
+        side = jnp.concatenate(moved, axis=0).astype(jnp.bfloat16)
+        buf_ref[r * KR : (r + 1) * KR, lane : lane + CH] = jnp.dot(
+            flipped, side, preferred_element_type=jnp.float32
+        )
+
+
+def rounded(values):
+    return values.astype(jnp.bfloat16).astype(jnp.float32)
+
+
+def taps_of(parts):
+    return jnp.concatenate([stack_taps(side_taps(n * g)) for n, g, _ in parts], axis=0)
+
+
+def forward_rows(inputs, bias_ref, w1_ref, w2_ref, same_group):
+    parts_a = [norm_parts(v, same_group) for v in inputs]
+    taps_a = taps_of(parts_a)
+    mids = conv_rows(taps_a, w1_ref)
+    mids = [mid + bias_ref[i : i + 1, :] for i, mid in enumerate(mids)]
+    parts_b = [norm_parts(v, same_group) for v in mids]
+    taps_b = taps_of(parts_b)
+    outs = conv_rows(taps_b, w2_ref)
+    return mids, [v + o for v, o in zip(inputs, outs)], parts_a, taps_a, parts_b, taps_b
+
+
+def backward_rows(grads, kept, emb_ref, w1_ref, w2_ref, same_group, buf_ref):
+    parts_a, taps_a, parts_b, taps_b = kept
+    low = [rounded(g) for g in grads]
+    weight_rows(taps_b, low, buf_ref, CH)
+    back = conv_rows_back(low, w2_ref)
+    grad_mid = [norm_back(p, b, same_group) for p, b in zip(parts_b, back)]
+    d_time = None
+    for i, gm in enumerate(grad_mid):
+        part = emb_ref[:, i : i + 1] * col_sum(gm)
+        d_time = part if d_time is None else d_time + part
+    buf_ref[9 * CH : 9 * CH + TE // 2, 0:CH] = d_time[: TE // 2]
+    buf_ref[9 * CH : 9 * CH + TE // 2, CH : 2 * CH] = d_time[TE // 2 :]
+    pad = buf_ref.shape[0] - 9 * CH - TE // 2
+    buf_ref[9 * CH + TE // 2 :, :] = jnp.zeros((pad, 2 * CH), jnp.float32)
+    low = [rounded(g) for g in grad_mid]
+    weight_rows(taps_a, low, buf_ref, 0)
+    back = conv_rows_back(low, w1_ref)
+    return [g + norm_back(p, b, same_group) for g, p, b in zip(grads, parts_a, back)]
+
+
+def put_images(ref, images):
+    for i, image in enumerate(images):
+        ref[i * PIX : (i + 1) * PIX, :] = image
+
+
+def first_kernel(x_ref, bias_ref, w1_ref, w2_ref, same_ref, mid_ref, y_ref):
+    inputs = images_of(x_ref[...].astype(jnp.float32))
+    mids, outs, *_ = forward_rows(inputs, bias_ref, w1_ref, w2_ref, same_ref[...])
+    put_images(mid_ref, mids)
+    put_images(y_ref, outs)
+
+
+def last_kernel(y_ref, target_ref, bias_ref, emb_ref, w1_ref, w2_ref, same_ref, gu_ref, buf_ref):
+    same = same_ref[...]
+    inputs = [y + y for y in images_of(y_ref[...])]
+    _, outs, *kept = forward_rows(inputs, bias_ref, w1_ref, w2_ref, same)
+    wanted = images_of(target_ref[...].astype(jnp.float32))
+    scale = 1.0 / math.sqrt(PIX)
+    grads = [(o - w) * scale for o, w in zip(outs, wanted)]
+    put_images(gu_ref, backward_rows(grads, kept, emb_ref, w1_ref, w2_ref, same, buf_ref))
+
+
+def return_kernel(x_ref, mid_ref, gu_ref, emb_ref, w1_ref, w2_ref, same_ref, buf_ref):
+    same = same_ref[...]
+    parts_a = [norm_parts(v, same) for v in images_of(x_ref[...].astype(jnp.float32))]
+    parts_b = [norm_parts(v, same) for v in images_of(mid_ref[...])]
+    kept = (parts_a, taps_of(parts_a), parts_b, taps_of(parts_b))
+    grads = [g + g for g in images_of(gu_ref[...])]
+    backward_rows(grads, kept, emb_ref, w1_ref, w2_ref, same, buf_ref)
+
+
+def in_vmem(kernel, name, outs):
+    return pl.pallas_call(
+        kernel,
+        name=name,
+        out_shape=outs,
+        compiler_params=pltpu.CompilerParams(vmem_limit_bytes=VMEM_BYTES),
+    )
+
+
+def buffer_rows(replicas):
+    step = 8 * 2 * replicas
+    return -(-(9 * CH + TE // 2) // step) * step
+
+
+def local_two(features, target, timesteps, conv_one, conv_two, time_proj):
+    section_pos = lax.axis_index("section")
+    images = features.shape[0]
+    rows = images * PIX
+    x = features.reshape(rows, CH)
+    wanted = target.reshape(rows, CH)
+    w1, w2 = conv_one[0], conv_two[0]
+    embedded = embed_times(timesteps)
+    bias = jnp.dot(embedded, time_proj[0], precision=lax.Precision.HIGHEST)
+    emb = embedded.T
+    group = jnp.arange(CH) // (CH // GROUPS)
+    same = (group[:, None] == group[None, :]).astype(jnp.float32)
+    flat = jax.ShapeDtypeStruct((rows, CH), jnp.float32)
+    packed_rows = buffer_rows(lax.axis_size("dp"))
+    packed = jax.ShapeDtypeStruct((packed_rows, 2 * CH), jnp.float32)
+
+    def blank(shape):
+        return jnp.zeros(shape.shape, shape.dtype)
+
+    mid, y = lax.cond(
+        section_pos == 0,
+        lambda: tuple(in_vmem(first_kernel, "first", [flat, flat])(x, bias, w1, w2, same)),
+        lambda: (blank(flat), blank(flat)),
+    )
+    y = lax.ppermute(y, "section", [(0, 1)])
+    gu, buf = lax.cond(
+        section_pos == 1,
+        lambda: tuple(
+            in_vmem(last_kernel, "last", [flat, packed])(y, wanted, bias, emb, w1, w2, same)
+        ),
+        lambda: (blank(flat), blank(packed)),
+    )
+    gu = lax.ppermute(gu, "section", [(1, 0)])
+    buf = lax.cond(
+        section_pos == 0,
+        lambda: in_vmem(return_kernel, "back", packed)(x, mid, gu, emb, w1, w2, same),
+        lambda: buf,
+    )
+    buf = sum_over_dp(buf)
+    d_time = jnp.concatenate(
+        [buf[9 * CH : 9 * CH + TE // 2, :CH], buf[9 * CH : 9 * CH + TE // 2, CH:]], axis=0
+    )
+    return (buf[None, : 9 * CH, :CH], buf[None, : 9 * CH, CH:], d_time[None])
+
+
+def sum_over_dp(buf):
+    return lax.psum(buf, "dp")
+
+
 def solution(mesh):
     placed = (
         P("dp", None, None),
@@ -264,8 +501,9 @@
         P("section", None, None),
         P("section", None, None),
     )
+    body = local_two if mesh.shape["section"] == 2 else local
     return jax.shard_map(
-        local,
+        body,
         mesh=mesh,
         in_specs=placed,
         out_specs=(P("section", None, None), P("section", None, None), P("section", None, None)),

time: 746 us -> 298 us (0.40)
  local copies, waits for them, and re-layouts: 211 us -> 39.8 us
  starting transfers between devices: 159 us -> 3.45 us
  other arithmetic: 122 us -> 1.18 us
  matrix products: 39.7 us -> 0.37 us
  waiting for transfers between devices: 186 us -> 214 us
  Pallas kernels: 0 us -> 23.8 us
  loops' own time: 9.1 us -> 0.02 us
    ppermute x12 -> x2, starting transfers between devices: 159 us -> 3.41 us  [the longest x1 2.13 us: local_two(): y = lax.ppermute(y, 'section', [(0, 1)])]
    scatter-add x28 -> x0, local copies, waits for them, and re-layouts: 105 us -> none  [conv_back(): padded.at[:, row_shift:row_shift + height, col_shift:col_shift + width, :]]
    add x31 -> x0, other arithmetic: 56.5 us -> none  [the longest x3 25.9 us: backward_tick(): total_two + delta_two]
    dot_general x15 -> x1, matrix products: 39.7 us -> 0.37 us  [local_two(): bias = jnp.dot(embedded, time_proj[0], precision=lax.Precision.HIGHEST)]
    concatenate x14 -> x0, local copies, waits for them, and re-layouts: 36.9 us -> none  [patches(): return jnp.concatenate(taps, axis=-1)]
    ppermute x12 -> x2, waiting for transfers between devices: 14.9 us -> 51.1 us  [the longest x1 37.4 us: local_two(): gu = lax.ppermute(gu, 'section', [(1, 0)])]
    pallas_call x0 -> x2, Pallas kernels: none -> 23.8 us  [the longest x1 14.8 us: local_two(): in_vmem(return_kernel, 'back', packed)(x, mid, gu, emb, w1, w2, same)]
    dynamic_update_slice x12 -> x0, other arithmetic: 17.6 us -> none  [put_slot(): return lax.dynamic_update_index_in_dim(buffer, fresh, slot, 0)]
  transfers between devices with their start and end apart: 13 -> 3, of which waited for: 8 -> 3; matrix products, arithmetic and copies ran while one was open for 7% -> 0% of each run, Pallas kernels for 0% -> 0%
where the time goes in v1:
time: 298 us; the launch traced here: 297 us
  waiting for transfers between devices  214 us (72%)
  local copies, waits for them, and re-layouts  39.8 us (13%)
  Pallas kernels  23.8 us (8%)
  between operations  14.1 us (5%)
  starting transfers between devices  3.45 us (1%)
    psum x1, waiting for transfers between devices, sum_over_dp(): return lax.psum(buf, 'dp')  163 us
    ppermute x1, waiting for transfers between devices, local_two(): gu = lax.ppermute(gu, 'section', [(1, 0)])  37.4 us
    pallas_call x1, Pallas kernels, local_two(): in_vmem(return_kernel, 'back', packed)(x, mid, gu, emb, w1, w2, same)  14.8 us
    ppermute x1, waiting for transfers between devices, local_two(): y = lax.ppermute(y, 'section', [(0, 1)])  13.7 us
    cond x1, local copies, waits for them, and re-layouts, local_two(): lax.cond(section_pos == 0, lambda: in_vmem(return_kernel, 'back', packed)...  9.07 us
    pallas_call x1, Pallas kernels, local_two(): in_vmem(first_kernel, 'first', [flat, flat])(x, bias, w1, w2, same)  9.02 us
    unnamed x7, local copies, waits for them, and re-layouts  8.34 us
    another operation x4, local copies, waits for them, and re-layouts  7.72 us
  transfers between devices with their start and end apart: 3, of which 3 were waited for; matrix products, arithmetic and copies ran while one was open for 0% of the time, Pallas kernels for 0%

profile of v1, /device:TPU:1, one launch (start us, length us, event | category | flops | bytes accessed | tf_op | source)
XLA Modules:
  0.0 296.6 jit_solution(12311571175307475008)
XLA Ops:
  7.3 0.7 convert_element_type.19
  8.0 2.1 reshape.45
  10.2 3.3 %copy.16 = bf16[1,2880,320]{2,1,0:T(8,128)(2,1)S(1)} copy(bf16[1,2880,320]{1,2,0:T(8,128)(2,1)} %param.15) | data formatting | bytes 3686400 | tf_op args[3]
  13.5 4.0 %copy.17 = bf16[1,2880,320]{2,1,0:T(8,128)(2,1)} copy(bf16[1,2880,320]{1,2,0:T(8,128)(2,1)} %param.16) | data formatting | bytes 3686400 | tf_op args[4]
  18.0 9.0 %conditional.3 = ((f32[512,320]{1,0:T(8,128)}, f32[512,320]{1,0:T(8,128)})) conditional(s32[]{:T(128)} %convert_element_type.17, () %tuple.33, (bf16[512,320]{1,0:T(8,128)(2,1)}, f32[2,320]{1,0:T(2,128)S(1)}, bf16[2880,320]{1,0:T(8,128)(2,1)S(1)}, bf16[2880,320]{1,0:T(8,128)(2,1)}, f32[320,320]{1,0:T(8,128)S(1)}) %tuple.60), branch_computations={%region_0.1_spmd, %region_1.2_spmd} | conditional | bytes 1310752 | solution.py:465
  18.0 9.0 %first.1 = (f32[512,320]{1,0:T(8,128)}, f32[512,320]{1,0:T(8,128)}) custom-call(bf16[512,320]{1,0:T(8,128)(2,1)} %get-tuple-element.46.x_ref, f32[2,320]{1,0:T(2,128)S(1)} %get-tuple-element.47.bias_ref, bf16[2880,320]{1,0:T(8,128)(2,1)S(1)} %get-tuple-element.48.w1_ref, bf16[2880,320]{1,0:T(8,128)(2,1)} %get-tuple-element.49.w2_ref, ...), custom_call_target="tpu_custom_call" | custom-call | tf_op jit(solution)/shard_map/cond/branch_1_fun/first/pallas_call | solution.py:467
  27.0 2.2 copy.18
  29.3 2.1 collective-permute-start
  31.5 13.7 %collective-permute-done = f32[512,320]{0,1:T(8,128)} collective-permute-done((f32[512,320]{0,1:T(8,128)}, f32[512,320]{0,1:T(8,128)}, u32[]{:S(2)}, u32[]{:S(2)}) %collective-permute-start) | collective-permute-done | bytes 655392 | tf_op jit(solution)/shard_map/ppermute | solution.py:470
  45.2 4.6 %conditional.4 = ((f32[512,320]{1,0:T(8,128)}, f32[3072,640]{1,0:T(8,128)})) conditional(s32[]{:T(128)} %convert_element_type.18, () %tuple.32, (bf16[2,16,5120]{2,1,0:T(8,128)(2,1)S(1)}, f32[512,320]{0,1:T(8,128)}, f32[2,320]{1,0:T(2,128)S(1)}, f32[320,2]{0,1:T(2,128)S(1)}, bf16[2880,320]{1,0:T(8,128)(2,1)S(1)}, ...), branch_computations={%region_2.3_spmd, %region_3.4_spmd} | conditional | bytes 8519712 | solution.py:471
  45.2 1.0 broadcast.57
  46.2 3.7 %broadcast.58 = f32[3072,640]{1,0:T(8,128)} broadcast(f32[]{:T(128)} %constant.8.clone), dimensions={} | broadcast | bytes 7864324 | tf_op jit(solution)/shard_map/broadcast.4
  49.8 2.2 copy.21
  52.1 1.3 collective-permute-start.1
  53.4 37.4 %collective-permute-done.1 = f32[512,320]{0,1:T(8,128)} collective-permute-done((f32[512,320]{0,1:T(8,128)}, f32[512,320]{0,1:T(8,128)}, u32[]{:S(2)}, u32[]{:S(2)}) %collective-permute-start.1) | collective-permute-done | bytes 655392 | tf_op jit(solution)/shard_map/ppermute | solution.py:478
  90.7 17.9 %conditional.5 = (f32[3072,640]{1,0:T(8,128)}) conditional(s32[]{:T(128)} %convert_element_type.17, f32[3072,640]{1,0:T(8,128)} %get-tuple-element.73, (bf16[512,320]{1,0:T(8,128)(2,1)}, f32[512,320]{1,0:T(8,128)}, f32[512,320]{0,1:T(8,128)}, f32[320,2]{0,1:T(2,128)S(1)}, bf16[2880,320]{1,0:T(8,128)(2,1)S(1)}, /*index=5*/bf16[2880,320]{1,0:T(8,128)(2,1)}, ...), branch_computations={%region_4.5_spmd, %region_5.6_spmd} | conditional | bytes 1315848 | solution.py:479
  90.7 0.8 copy.23.emb_ref
  91.6 2.3 copy.22.gu_ref
  93.8 14.8 %back.1 = f32[3072,640]{1,0:T(8,128)} custom-call(bf16[512,320]{1,0:T(8,128)(2,1)} %get-tuple-element.58.x_ref, f32[512,320]{1,0:T(8,128)} %get-tuple-element.59.mid_ref, f32[512,320]{1,0:T(8,128)} %copy.22.gu_ref, f32[320,2]{1,0:T(8,128)} %copy.23.emb_ref, bf16[2880,320]{1,0:T(8,128)(2,1)S(1)} %get-tuple-element.62.w1_ref, ...), custom_call_target="tpu_custom_call" | custom-call | tf_op jit(solution)/shard_map/cond/branch_1_fun/back/pallas_call | solution.py:481
  108.6 9.1 %copy.24 = f32[3072,640]{0,1:T(8,128)} copy(f32[3072,640]{1,0:T(8,128)} %get-tuple-element.114) | data formatting | bytes 15728640 | tf_op jit(solution)/shard_map/cond | solution.py:479
  117.7 162.8 %all-reduce.2.cloned.1.call-done = f32[3072,640]{0,1:T(8,128)} async-done(((f32[3072,640]{0,1:T(8,128)}), f32[3072,640]{0,1:T(8,128)}) %all-reduce.2.cloned.1.call-update) | async-done | bytes 7864336 | tf_op jit(solution)/shard_map/psum | solution.py:492
  280.5 1.3 fusion.7
  282.0 1.0 copy.25
  283.0 6.8 %slice_bitcast_fusion = (f32[1,2880,320]{1,2,0:T(8,128)}, f32[1,2880,320]{1,2,0:T(8,128)}) fusion(f32[3072,640]{0,1:T(8,128)} %all-reduce.2.cloned.1.call-done), kind=kLoop, calls=%fused_computation | loop fusion | bytes 14745600 | tf_op jit(solution)/shard_map/broadcast_in_dim | solution.py:488
  (13 shorter events, 0.9 us)
Async XLA Ops:
  7.2 10.5 %copy-start = (f32[1,320,320]{2,1,0:T(8,128)S(1)}, f32[1,320,320]{2,1,0:T(8,128)}, u32[]{:S(2)}) copy-start(f32[1,320,320]{2,1,0:T(8,128)} %param.17) | copy-start | bytes 1228804
  7.2 273.3 %all-reduce.2.cloned.1.call-start = ((), (), s32[]{:S(2)}) async-start(), calls=%async_computation | async-start | bytes 15728640 | tf_op jit(solution)/shard_map/psum | solution.py:492
  10.2 35.0 %copy-start.1 = (bf16[2,16,5120]{2,1,0:T(8,128)(2,1)S(1)}, bf16[2,16,5120]{2,1,0:T(8,128)(2,1)}, u32[]{:S(2)}) copy-start(bf16[2,16,5120]{2,1,0:T(8,128)(2,1)} %param.13) | copy-start | bytes 983044
  29.3 15.9 %collective-permute-start = (f32[512,320]{0,1:T(8,128)}, f32[512,320]{0,1:T(8,128)}, u32[]{:S(2)}, u32[]{:S(2)}) collective-permute-start(f32[512,320]{0,1:T(8,128)} %copy.18), channel_id=1, source_target_pairs={{0,1},{2,3},{4,5},{6,7},{8,9},{10,11},{12,13},{14,15},{16,17},{18,... | collective-permute-start | bytes 1966088 | tf_op jit(solution)/shard_map/ppermute | solution.py:470
  52.1 38.7 %collective-permute-start.1 = (f32[512,320]{0,1:T(8,128)}, f32[512,320]{0,1:T(8,128)}, u32[]{:S(2)}, u32[]{:S(2)}) collective-permute-start(f32[512,320]{0,1:T(8,128)} %copy.21), channel_id=1, source_target_pairs={{1,0},{3,2},{5,4},{7,6},{9,8},{11,10},{13,12},{15,14},{17,16},{19,... | collective-permute-start | bytes 1966088 | tf_op jit(solution)/shard_map/ppermute | solution.py:478
Sparse Core Ops, SparseCore 0:
  117.9 162.6 all-reduce.1

commit v2 on v1

--- a/solution.py
+++ b/solution.py
@@ -439,7 +439,7 @@
 
 
 def buffer_rows(replicas):
-    step = 8 * 2 * replicas
+    step = 8 * replicas * SUBS
     return -(-(9 * CH + TE // 2) // step) * step
 
 
@@ -488,8 +488,139 @@
     return (buf[None, : 9 * CH, :CH], buf[None, : 9 * CH, CH:], d_time[None])
 
 
+CORES = 2
+CHIPS = 8
+SUBS = 2
+
+
+def ring_places():
+    dp = lax.axis_index("dp")
+    core = dp % CORES
+    chip = dp // CORES
+    x, z = chip % 2, chip // 2
+    place = z + x * (CHIPS - 1 - 2 * z)
+    way = 1 - 2 * core
+
+    def device(at):
+        side = at // (CHIPS // 2)
+        depth = at + side * (CHIPS - 1 - 2 * at)
+        return {"dp": (depth * 2 + side) * CORES + core}
+
+    after = device((place + way + CHIPS) % CHIPS)
+    before = device((place - way + CHIPS) % CHIPS)
+    sibling = {"dp": chip * CORES + 1 - core}
+    return core, place, way, after, before, sibling
+
+
+def ring_meet(after, before, sibling):
+    barrier = pltpu.get_barrier_semaphore()
+    for other in (after, before, sibling):
+        pl.semaphore_signal(barrier, inc=1, device_id=other, device_id_type=MESH_IDS)
+    pl.semaphore_wait(barrier, 3)
+
+
+def ring_kernel(in_ref, out_ref, pair_ref, slot_ref, work_ref, pair_sems, step_sems, turn_sems, give_sems):
+    core, place, way, after, before, sibling = ring_places()
+    ring_meet(after, before, sibling)
+
+    def remote(src, dst, sems, index, target):
+        return pltpu.make_async_remote_copy(
+            src_ref=src,
+            dst_ref=dst,
+            send_sem=sems.at[(0,) + index],
+            recv_sem=sems.at[(1,) + index],
+            device_id=target,
+            device_id_type=MESH_IDS,
+        )
+
+    def block_at(step):
+        return (place - way * step + 2 * CHIPS) % CHIPS
+
+    def sibling_block_at(step):
+        return (place + way * step + 2 * CHIPS) % CHIPS
+
+    pending = []
+    pairs = {}
+    for step in range(CHIPS):
+        for sub in range(SUBS):
+            theirs = sibling_block_at(step)
+            copy = remote(
+                in_ref.at[1 - core, theirs, sub], pair_ref.at[step, sub], pair_sems, (step, sub), sibling
+            )
+            copy.start()
+            pairs[step, sub] = copy
+            pending.append(copy)
+
+    arrived = {}
+    for step in range(CHIPS):
+        for sub in range(SUBS):
+            block = block_at(step)
+            pairs[step, sub].wait_recv()
+            total = in_ref[core, block, sub] + pair_ref[step, sub]
+            if step:
+                arrived[step - 1, sub].wait_recv()
+                total = total + slot_ref[step - 1, sub]
+            if step < CHIPS - 1:
+                work_ref[step, sub] = total
+                copy = remote(
+                    work_ref.at[step, sub], slot_ref.at[step, sub], step_sems, (step, sub), after
+                )
+                copy.start()
+                arrived[step, sub] = copy
+                pending.append(copy)
+            else:
+                out_ref[core, block, sub] = total
+
+    turned = {}
+    gifts = []
+    for step in range(CHIPS):
+        for sub in range(SUBS):
+            block = block_at(CHIPS - 1 + step)
+            if step:
+                turned[step - 1, sub].wait_recv()
+            here = out_ref.at[core, block, sub]
+            if step < CHIPS - 1:
+                copy = remote(here, here, turn_sems, (step, sub), after)
+                copy.start()
+                turned[step, sub] = copy
+                pending.append(copy)
+            copy = remote(here, here, give_sems, (step, sub), sibling)
+            copy.start()
+            gifts.append(copy)
+    for copy in gifts:
+        copy.wait_recv()
+    for copy in pending + gifts:
+        copy.wait_send()
+
+
+def ring_scratch(part, lanes):
+    return [
+        pltpu.VMEM((CHIPS, SUBS, part, lanes), jnp.float32),
+        pltpu.VMEM((CHIPS - 1, SUBS, part, lanes), jnp.float32),
+        pltpu.VMEM((CHIPS - 1, SUBS, part, lanes), jnp.float32),
+        pltpu.SemaphoreType.DMA((2, CHIPS, SUBS)),
+        pltpu.SemaphoreType.DMA((2, CHIPS - 1, SUBS)),
+        pltpu.SemaphoreType.DMA((2, CHIPS - 1, SUBS)),
+        pltpu.SemaphoreType.DMA((2, CHIPS, SUBS)),
+    ]
+
+
 def sum_over_dp(buf):
-    return lax.psum(buf, "dp")
+    if lax.axis_size("dp") != CORES * CHIPS:
+        return lax.psum(buf, "dp")
+    rows, lanes = buf.shape
+    part = rows // (CORES * CHIPS * SUBS)
+    parts = (CORES, CHIPS, SUBS, part, lanes)
+    total = pl.pallas_call(
+        ring_kernel,
+        name="ring",
+        out_shape=jax.ShapeDtypeStruct(parts, jnp.float32),
+        scratch_shapes=ring_scratch(part, lanes),
+        compiler_params=pltpu.CompilerParams(
+            collective_id=0, has_side_effects=True, vmem_limit_bytes=VMEM_BYTES
+        ),
+    )(buf.reshape(parts))
+    return total.reshape(rows, lanes)
 
 
 def solution(mesh):

time: 298 us -> 225 us (0.76)
  waiting for transfers between devices: 214 us -> 61.9 us
  Pallas kernels: 23.8 us -> 116 us
  between operations: 14.1 us -> 0.73 us
    psum x1 -> x0, waiting for transfers between devices: 163 us -> none  [sum_over_dp(): return lax.psum(buf, 'dp')]
    pallas_call x0 -> x1, Pallas kernels: none -> 92.3 us  [sum_over_dp(): pl.pallas_call(ring_kernel, name='ring', out_shape=jax.ShapeDtypeStruct(p...]
    ppermute x1, waiting for transfers between devices: 37.4 us -> 48.2 us  [local_two(): gu = lax.ppermute(gu, 'section', [(1, 0)])]
    unnamed x7 -> x8, local copies, waits for them, and re-layouts: 8.34 us -> 18.5 us
    cond x1 -> x0, local copies, waits for them, and re-layouts: 9.07 us -> none  [local_two(): lax.cond(section_pos == 0, lambda: in_vmem(return_kernel, 'back', packed)...]
    slice x0 -> x1, local copies, waits for them, and re-layouts: none -> 8.21 us  [local_two(): return (buf[None, :9 * CH, :CH], buf[None, :9 * CH, CH:], d_time[None])]
    broadcast_in_dim x1 -> x0, local copies, waits for them, and re-layouts: 6.82 us -> none  [local_two(): return (buf[None, :9 * CH, :CH], buf[None, :9 * CH, CH:], d_time[None])]
  transfers between devices with their start and end apart: 3 -> 2, of which waited for: 3 -> 2; matrix products, arithmetic and copies ran while one was open for 0% -> 0% of each run, Pallas kernels for 0% -> 0%
where the time goes in v2:
time: 225 us; the launch traced here: 226 us
  Pallas kernels  116 us (52%)
  waiting for transfers between devices  61.9 us (28%)
  local copies, waits for them, and re-layouts  42.1 us (19%)
  starting transfers between devices  3.42 us (2%)
    pallas_call x1, Pallas kernels, sum_over_dp(): pl.pallas_call(ring_kernel, name='ring', out_shape=jax.ShapeDtypeStruct(p...  92.3 us
    ppermute x1, waiting for transfers between devices, local_two(): gu = lax.ppermute(gu, 'section', [(1, 0)])  48.2 us
    unnamed x8, local copies, waits for them, and re-layouts  18.5 us
    pallas_call x1, Pallas kernels, local_two(): in_vmem(return_kernel, 'back', packed)(x, mid, gu, emb, w1, w2, same)  14.8 us
    ppermute x1, waiting for transfers between devices, local_two(): y = lax.ppermute(y, 'section', [(0, 1)])  13.7 us
    pallas_call x1, Pallas kernels, local_two(): in_vmem(first_kernel, 'first', [flat, flat])(x, bias, w1, w2, same)  9 us
    slice x1, local copies, waits for them, and re-layouts, local_two(): return (buf[None, :9 * CH, :CH], buf[None, :9 * CH, CH:], d_time[None])  8.21 us
    another operation x4, local copies, waits for them, and re-layouts  7.73 us
  transfers between devices with their start and end apart: 2, of which 2 were waited for; matrix products, arithmetic and copies ran while one was open for 0% of the time, Pallas kernels for 0%

profile of v2, /device:TPU:1, one launch (start us, length us, event | category | flops | bytes accessed | tf_op | source)
XLA Modules:
  0.0 226.5 jit_solution(15047453458916565792)
XLA Ops:
  1.4 2.1 reshape.51
  3.6 3.3 %copy.16 = bf16[1,2880,320]{2,1,0:T(8,128)(2,1)S(1)} copy(bf16[1,2880,320]{1,2,0:T(8,128)(2,1)} %param.15) | data formatting | bytes 3686400 | tf_op args[3]
  6.9 4.0 %copy.17 = bf16[1,2880,320]{2,1,0:T(8,128)(2,1)} copy(bf16[1,2880,320]{1,2,0:T(8,128)(2,1)} %param.16) | data formatting | bytes 3686400 | tf_op args[4]
  11.4 9.0 %conditional.3 = ((f32[512,320]{1,0:T(8,128)}, f32[512,320]{1,0:T(8,128)})) conditional(s32[]{:T(128)} %convert_element_type.17, () %tuple.33, (bf16[512,320]{1,0:T(8,128)(2,1)}, f32[2,320]{1,0:T(2,128)S(1)}, bf16[2880,320]{1,0:T(8,128)(2,1)S(1)}, bf16[2880,320]{1,0:T(8,128)(2,1)}, f32[320,320]{1,0:T(8,128)S(1)}) %tuple.56), branch_computations={%region_0.1_spmd, %region_1.2_spmd} | conditional | bytes 1310752 | solution.py:465
  11.4 9.0 %first.1 = (f32[512,320]{1,0:T(8,128)}, f32[512,320]{1,0:T(8,128)}) custom-call(bf16[512,320]{1,0:T(8,128)(2,1)} %get-tuple-element.46.x_ref, f32[2,320]{1,0:T(2,128)S(1)} %get-tuple-element.47.bias_ref, bf16[2880,320]{1,0:T(8,128)(2,1)S(1)} %get-tuple-element.48.w1_ref, bf16[2880,320]{1,0:T(8,128)(2,1)} %get-tuple-element.49.w2_ref, ...), custom_call_target="tpu_custom_call" | custom-call | tf_op jit(solution)/shard_map/cond/branch_1_fun/first/pallas_call | solution.py:467
  20.4 2.2 copy.18
  22.6 2.1 collective-permute-start
  24.8 13.7 %collective-permute-done = f32[512,320]{0,1:T(8,128)} collective-permute-done((f32[512,320]{0,1:T(8,128)}, f32[512,320]{0,1:T(8,128)}, u32[]{:S(2)}, u32[]{:S(2)}) %collective-permute-start) | collective-permute-done | bytes 655392 | tf_op jit(solution)/shard_map/ppermute | solution.py:470
  38.5 4.6 %conditional.4 = ((f32[512,320]{1,0:T(8,128)}, f32[3072,640]{1,0:T(8,128)})) conditional(s32[]{:T(128)} %convert_element_type.18, () %tuple.32, (bf16[2,16,5120]{2,1,0:T(8,128)(2,1)S(1)}, f32[512,320]{0,1:T(8,128)}, f32[2,320]{1,0:T(2,128)S(1)}, f32[320,2]{0,1:T(2,128)S(1)}, bf16[2880,320]{1,0:T(8,128)(2,1)S(1)}, ...), branch_computations={%region_2.3_spmd, %region_3.4_spmd} | conditional | bytes 8519712 | solution.py:471
  38.5 1.0 broadcast.57
  39.5 3.7 %broadcast.58 = f32[3072,640]{1,0:T(8,128)} broadcast(f32[]{:T(128)} %constant.8.clone), dimensions={} | broadcast | bytes 7864324 | tf_op jit(solution)/shard_map/broadcast.4
  43.2 2.2 copy.21
  45.4 1.3 collective-permute-start.1
  46.7 48.2 %collective-permute-done.1 = f32[512,320]{0,1:T(8,128)} collective-permute-done((f32[512,320]{0,1:T(8,128)}, f32[512,320]{0,1:T(8,128)}, u32[]{:S(2)}, u32[]{:S(2)}) %collective-permute-start.1) | collective-permute-done | bytes 655392 | tf_op jit(solution)/shard_map/ppermute | solution.py:478
  94.9 17.9 %conditional.5 = (f32[3072,640]{1,0:T(8,128)}) conditional(s32[]{:T(128)} %convert_element_type.17, f32[3072,640]{1,0:T(8,128)} %get-tuple-element.73, (bf16[512,320]{1,0:T(8,128)(2,1)}, f32[512,320]{1,0:T(8,128)}, f32[512,320]{0,1:T(8,128)}, f32[320,2]{0,1:T(2,128)S(1)}, bf16[2880,320]{1,0:T(8,128)(2,1)S(1)}, /*index=5*/bf16[2880,320]{1,0:T(8,128)(2,1)}, ...), branch_computations={%region_4.5_spmd, %region_5.6_spmd} | conditional | bytes 1315848 | solution.py:479
  94.9 0.8 copy.23.emb_ref
  95.7 2.3 %copy.22.gu_ref = f32[512,320]{1,0:T(8,128)} copy(f32[512,320]{0,1:T(8,128)} %get-tuple-element.87) | data formatting | bytes 1310720 | tf_op jit(solution)/shard_map
  98.0 14.8 %back.1 = f32[3072,640]{1,0:T(8,128)} custom-call(bf16[512,320]{1,0:T(8,128)(2,1)} %get-tuple-element.58.x_ref, f32[512,320]{1,0:T(8,128)} %get-tuple-element.59.mid_ref, f32[512,320]{1,0:T(8,128)} %copy.22.gu_ref, f32[320,2]{1,0:T(8,128)} %copy.23.emb_ref, bf16[2880,320]{1,0:T(8,128)(2,1)S(1)} %get-tuple-element.62.w1_ref, ...), custom_call_target="tpu_custom_call" | custom-call | tf_op jit(solution)/shard_map/cond/branch_1_fun/back/pallas_call | solution.py:481
  112.8 92.3 %ring.1 = f32[2,8,2,96,640]{4,3,2,1,0:T(8,128)} custom-call(f32[2,8,2,96,640]{4,3,2,1,0:T(8,128)} %bitcast.21), custom_call_target="tpu_custom_call" | custom-call | tf_op jit(solution)/shard_map/ring/pallas_call | solution.py:614
  205.1 1.2 fusion.7
  206.3 8.2 %fusion.8 = (f32[2880,320]{1,0:T(8,128)}, f32[2880,320]{1,0:T(8,128)}) fusion(f32[3072,640]{1,0:T(8,128)} %bitcast.14), kind=kLoop, calls=%fused_computation.18 | loop fusion | bytes 14745600 | tf_op jit(solution)/shard_map/slice | solution.py:488
  214.5 5.6 %copy.27 = f32[2880,320]{0,1:T(8,128)} copy(f32[2880,320]{1,0:T(8,128)} %get-tuple-element.94) | data formatting | bytes 7372800
  220.1 5.6 %copy.26 = f32[2880,320]{0,1:T(8,128)} copy(f32[2880,320]{1,0:T(8,128)} %get-tuple-element.95) | data formatting | bytes 7372800
  225.7 0.8 maximum_bitcast_fusion
  (11 shorter events, 1.4 us)
Async XLA Ops:
  0.6 10.4 %copy-start = (f32[1,320,320]{2,1,0:T(8,128)S(1)}, f32[1,320,320]{2,1,0:T(8,128)}, u32[]{:S(2)}) copy-start(f32[1,320,320]{2,1,0:T(8,128)} %param.17) | copy-start | bytes 1228804
  11.0 27.5 %copy-start.1 = (bf16[2,16,5120]{2,1,0:T(8,128)(2,1)S(1)}, bf16[2,16,5120]{2,1,0:T(8,128)(2,1)}, u32[]{:S(2)}) copy-start(bf16[2,16,5120]{2,1,0:T(8,128)(2,1)} %param.13) | copy-start | bytes 983044
  22.6 15.9 %collective-permute-start = (f32[512,320]{0,1:T(8,128)}, f32[512,320]{0,1:T(8,128)}, u32[]{:S(2)}, u32[]{:S(2)}) collective-permute-start(f32[512,320]{0,1:T(8,128)} %copy.18), channel_id=1, source_target_pairs={{0,1},{2,3},{4,5},{6,7},{8,9},{10,11},{12,13},{14,15},{16,17},{18,... | collective-permute-start | bytes 1966088 | tf_op jit(solution)/shard_map/ppermute | solution.py:470
  45.4 49.5 %collective-permute-start.1 = (f32[512,320]{0,1:T(8,128)}, f32[512,320]{0,1:T(8,128)}, u32[]{:S(2)}, u32[]{:S(2)}) collective-permute-start(f32[512,320]{0,1:T(8,128)} %copy.21), channel_id=1, source_target_pairs={{1,0},{3,2},{5,4},{7,6},{9,8},{11,10},{13,12},{15,14},{17,16},{19,... | collective-permute-start | bytes 1966088 | tf_op jit(solution)/shard_map/ppermute | solution.py:478

commit v3 on v0

--- a/solution.py
+++ b/solution.py
@@ -3,6 +3,8 @@
 import jax
 import jax.numpy as jnp
 from jax import lax
+from jax.experimental import pallas as pl
+from jax.experimental.pallas import tpu as pltpu
 from jax.sharding import PartitionSpec as P
 
 CH = 320
@@ -255,6 +257,339 @@
     return (sum_one[None], sum_two[None], sum_time[None])
 
 
+PIX = HEIGHT * WIDTH
+KR = 3 * CH
+MESH_IDS = pl.DeviceIdType.MESH
+VMEM_BYTES = 56 * 1024 * 1024
+
+
+def group_mean(cols, same_group):
+    wide = jnp.broadcast_to(cols, (8, CH))
+    total = jnp.dot(
+        wide, same_group, precision=lax.Precision.HIGHEST, preferred_element_type=jnp.float32
+    )
+    return total[0:1, :] * (1.0 / (PIX * (CH // GROUPS)))
+
+
+def col_sum(values):
+    return jnp.sum(values, axis=0, keepdims=True)
+
+
+def norm_parts(values, same_group):
+    centered = values - group_mean(col_sum(values), same_group)
+    inv = lax.rsqrt(group_mean(col_sum(centered * centered), same_group) + 1e-05)
+    normed = centered * inv
+    gate = 1.0 / (1.0 + jnp.exp(-normed))
+    return normed, gate, inv
+
+
+def norm_back(parts, cotangent, same_group):
+    normed, gate, inv = parts
+    dn = cotangent * (gate * (1.0 + normed * (1.0 - gate)))
+    mean_dn = group_mean(col_sum(dn), same_group)
+    mean_dnn = group_mean(col_sum(dn * normed), same_group)
+    return inv * (dn - mean_dn - normed * mean_dnn)
+
+
+def side_taps(values):
+    column = lax.broadcasted_iota(jnp.int32, (PIX, CH), 0) % WIDTH
+    before = jnp.where(column == 0, 0.0, pltpu.roll(values, 1, 0))
+    after = jnp.where(column == WIDTH - 1, 0.0, pltpu.roll(values, PIX - 1, 0))
+    return before, values, after
+
+
+def add_rows(low, mid, high):
+    edge = jnp.zeros((WIDTH, CH), jnp.float32)
+    down = jnp.concatenate([edge, low[: PIX - WIDTH]], axis=0)
+    up = jnp.concatenate([high[WIDTH:], edge], axis=0)
+    return down + mid + up
+
+
+def patch_rows(values):
+    taps = jnp.concatenate(side_taps(values), axis=1).astype(jnp.bfloat16)
+    edge = jnp.zeros((WIDTH, KR), jnp.bfloat16)
+    above = jnp.concatenate([edge, taps[: PIX - WIDTH]], axis=0)
+    below = jnp.concatenate([taps[WIDTH:], edge], axis=0)
+    return jnp.concatenate([above, taps, below], axis=1)
+
+
+def conv_rows_back(low, wt_ref):
+    spread = jnp.dot(low, wt_ref[...], preferred_element_type=jnp.float32)
+    cols = []
+    for c in range(3):
+        high, mid, down = [
+            spread[:, (3 * r + c) * CH : (3 * r + c + 1) * CH] for r in range(3)
+        ]
+        cols.append(add_rows(down, mid, high))
+    return side_taps(cols[2])[0] + cols[1] + side_taps(cols[0])[2]
+
+
+def weight_rows(patches_low, low, buf_ref, first):
+    buf_ref[first : first + CH, : 9 * CH] += jnp.dot(
+        low.T, patches_low, preferred_element_type=jnp.float32
+    )
+
+
+def taps_of(parts):
+    normed, gate, _ = parts
+    return patch_rows(normed * gate)
+
+
+def forward_rows(rows, bias, w1_ref, w2_ref, same_group):
+    parts_a = norm_parts(rows, same_group)
+    taps_a = taps_of(parts_a)
+    mid = jnp.dot(taps_a, w1_ref[...], preferred_element_type=jnp.float32) + bias
+    parts_b = norm_parts(mid, same_group)
+    taps_b = taps_of(parts_b)
+    out = rows + jnp.dot(taps_b, w2_ref[...], preferred_element_type=jnp.float32)
+    return mid, out, parts_a, taps_a, parts_b, taps_b
+
+
+def backward_rows(grad, kept, emb, wt1_ref, wt2_ref, same_group, buf_ref):
+    parts_a, taps_a, parts_b, taps_b = kept
+    low = grad.astype(jnp.bfloat16)
+    back = conv_rows_back(low, wt2_ref)
+    weight_rows(taps_b, low, buf_ref, CH)
+    grad_mid = norm_back(parts_b, back, same_group)
+    d_time = emb * col_sum(grad_mid)
+    half = CH // 2
+    buf_ref[0:TE, 9 * CH : 9 * CH + half] += d_time[:, :half]
+    buf_ref[TE : 2 * TE, 9 * CH : 9 * CH + half] += d_time[:, half:]
+    low = grad_mid.astype(jnp.bfloat16)
+    weight_rows(taps_a, low, buf_ref, 0)
+    back = conv_rows_back(low, wt1_ref)
+    return grad + norm_back(parts_a, back, same_group)
+
+
+CORES = 2
+CHIPS = 8
+BLOCK = 2 * CH // (CORES * CHIPS)
+SPLITS = ((0, 24), (24, 16))
+SUBS = len(SPLITS)
+LANES = 3072
+
+
+def ring_places():
+    dp = lax.axis_index("dp")
+    core = dp % CORES
+    chip = dp // CORES
+    x, z = chip % 2, chip // 2
+    place = z + x * (CHIPS - 1 - 2 * z)
+    way = 1 - 2 * core
+
+    def device(at):
+        side = at // (CHIPS // 2)
+        depth = at + side * (CHIPS - 1 - 2 * at)
+        return {"dp": (depth * 2 + side) * CORES + core}
+
+    after = device((place + way + CHIPS) % CHIPS)
+    before = device((place - way + CHIPS) % CHIPS)
+    sibling = {"dp": chip * CORES + 1 - core}
+    return core, place, way, after, before, sibling
+
+
+def meet(others):
+    barrier = pltpu.get_barrier_semaphore()
+    for other in others:
+        pl.semaphore_signal(barrier, inc=1, device_id=other, device_id_type=MESH_IDS)
+    pl.semaphore_wait(barrier, len(others))
+
+
+def ring_sum(places, in_ref, out_ref, pair_ref, slot_ref, work_ref, pair_sems, step_sems, turn_sems, give_sems):
+    core, place, way, after, before, sibling = places
+
+    def rows_of(half, block, sub):
+        first, size = SPLITS[sub]
+        start = (half * CHIPS + block) * BLOCK + first
+        return pl.ds(pl.multiple_of(start, 8), size)
+
+    def kept(ref, step, sub):
+        first, size = SPLITS[sub]
+        return ref.at[step, pl.ds(first, size)]
+
+    def remote(src, dst, sems, index, target):
+        return pltpu.make_async_remote_copy(
+            src_ref=src,
+            dst_ref=dst,
+            send_sem=sems.at[(0,) + index],
+            recv_sem=sems.at[(1,) + index],
+            device_id=target,
+            device_id_type=MESH_IDS,
+        )
+
+    def block_at(step):
+        return (place - way * step + 2 * CHIPS) % CHIPS
+
+    def sibling_block_at(step):
+        return (place + way * step + 2 * CHIPS) % CHIPS
+
+    pending = []
+    pairs = {}
+    for step in range(CHIPS):
+        for sub in range(SUBS):
+            theirs = sibling_block_at(step)
+            copy = remote(
+                in_ref.at[rows_of(1 - core, theirs, sub)], kept(pair_ref, step, sub), pair_sems, (step, sub), sibling
+            )
+            copy.start()
+            pairs[step, sub] = copy
+            pending.append(copy)
+
+    arrived = {}
+    for step in range(CHIPS):
+        for sub in range(SUBS):
+            block = block_at(step)
+            pairs[step, sub].wait_recv()
+            total = in_ref[rows_of(core, block, sub), :] + kept(pair_ref, step, sub)[...]
+            if step:
+                arrived[step - 1, sub].wait_recv()
+                total = total + kept(slot_ref, step - 1, sub)[...]
+            if step < CHIPS - 1:
+                kept(work_ref, step, sub)[...] = total
+                copy = remote(
+                    kept(work_ref, step, sub), kept(slot_ref, step, sub), step_sems, (step, sub), after
+                )
+                copy.start()
+                arrived[step, sub] = copy
+                pending.append(copy)
+            else:
+                out_ref[rows_of(core, block, sub), :] = total
+
+    turned = {}
+    gifts = []
+    for step in range(CHIPS):
+        for sub in range(SUBS):
+            block = block_at(CHIPS - 1 + step)
+            if step:
+                turned[step - 1, sub].wait_recv()
+            here = out_ref.at[rows_of(core, block, sub)]
+            if step < CHIPS - 1:
+                copy = remote(here, here, turn_sems, (step, sub), after)
+                copy.start()
+                turned[step, sub] = copy
+                pending.append(copy)
+            copy = remote(here, here, give_sems, (step, sub), sibling)
+            copy.start()
+            gifts.append(copy)
+    for copy in gifts:
+        copy.wait_recv()
+    for copy in pending + gifts:
+        copy.wait_send()
+
+
+def ring_scratch():
+    return [
+        pltpu.VMEM((CHIPS, BLOCK, LANES), jnp.float32),
+        pltpu.VMEM((CHIPS - 1, BLOCK, LANES), jnp.float32),
+        pltpu.VMEM((CHIPS - 1, BLOCK, LANES), jnp.float32),
+        pltpu.SemaphoreType.DMA((2, CHIPS, SUBS)),
+        pltpu.SemaphoreType.DMA((2, CHIPS - 1, SUBS)),
+        pltpu.SemaphoreType.DMA((2, CHIPS - 1, SUBS)),
+        pltpu.SemaphoreType.DMA((2, CHIPS, SUBS)),
+    ]
+
+
+def whole_kernel(
+    x_ref, target_ref, bias_ref, emb_ref, wt1_ref, wt2_ref, same_ref,
+    out_ref, w1_ref, w2_ref, mid_ref, send_ref, inbox_ref, buf_ref, send_sems, recv_sems, *ring_refs
+):
+    section = lax.axis_index("section")
+    places = ring_places()
+    partner = {"section": 1 - section}
+    meet(places[3:] + (partner,))
+    images = x_ref.shape[0]
+    w1_ref[...] = wt1_ref[...].T
+    w2_ref[...] = wt2_ref[...].T
+
+    def sent(i):
+        return pltpu.make_async_remote_copy(
+            src_ref=send_ref.at[i],
+            dst_ref=inbox_ref.at[i],
+            send_sem=send_sems.at[i],
+            recv_sem=recv_sems.at[i],
+            device_id=partner,
+            device_id_type=MESH_IDS,
+        )
+
+    @pl.when(section == 0)
+    def _():
+        @pl.loop(0, images)
+        def _(i):
+            rows = x_ref[i].astype(jnp.float32)
+            mid, out, *_ = forward_rows(rows, bias_ref[i], w1_ref, w2_ref, same_ref[...])
+            mid_ref[i] = mid
+            send_ref[i] = out
+            sent(i).start()
+
+    buf_ref[...] = jnp.zeros(buf_ref.shape, jnp.float32)
+
+    @pl.when(section == 0)
+    def _():
+        @pl.loop(0, images)
+        def _(i):
+            same = same_ref[...]
+            parts_a = norm_parts(x_ref[i].astype(jnp.float32), same)
+            parts_b = norm_parts(mid_ref[i], same)
+            kept = (parts_a, taps_of(parts_a), parts_b, taps_of(parts_b))
+            sent(i).wait_recv()
+            grad = inbox_ref[i] + inbox_ref[i]
+            backward_rows(grad, kept, emb_ref[i], wt1_ref, wt2_ref, same, buf_ref)
+
+    @pl.when(section == 1)
+    def _():
+        @pl.loop(0, images)
+        def _(i):
+            same = same_ref[...]
+            sent(i).wait_recv()
+            rows = inbox_ref[i] + inbox_ref[i]
+            _, out, *kept = forward_rows(rows, bias_ref[i], w1_ref, w2_ref, same)
+            grad = (out - target_ref[i].astype(jnp.float32)) * (1.0 / math.sqrt(PIX))
+            send_ref[i] = backward_rows(grad, kept, emb_ref[i], wt1_ref, wt2_ref, same, buf_ref)
+            sent(i).start()
+
+    for i in range(images):
+        sent(i).wait_send()
+    ring_sum(places, buf_ref, out_ref, *ring_refs)
+
+
+def local_two(features, target, timesteps, conv_one, conv_two, time_proj):
+    images = features.shape[0]
+    x = features.reshape(images, PIX, CH)
+    wanted = target.reshape(images, PIX, CH)
+    embedded = embed_times(timesteps)
+    bias = jnp.dot(embedded, time_proj[0], precision=lax.Precision.HIGHEST)
+    group = jnp.arange(CH) // (CH // GROUPS)
+    same = (group[:, None] == group[None, :]).astype(jnp.float32)
+    stack = pltpu.VMEM((images, PIX, CH), jnp.float32)
+    weight = pltpu.VMEM((9 * CH, CH), jnp.bfloat16)
+    total = pl.pallas_call(
+        whole_kernel,
+        name="whole",
+        out_shape=jax.ShapeDtypeStruct((2 * CH, LANES), jnp.float32),
+        in_specs=[pl.BlockSpec(memory_space=pltpu.VMEM)] * 7,
+        out_specs=pl.BlockSpec(memory_space=pltpu.VMEM),
+        scratch_shapes=[
+            weight,
+            weight,
+            stack,
+            stack,
+            stack,
+            pltpu.VMEM((2 * CH, LANES), jnp.float32),
+            pltpu.SemaphoreType.DMA((images,)),
+            pltpu.SemaphoreType.DMA((images,)),
+        ]
+        + ring_scratch(),
+        compiler_params=pltpu.CompilerParams(
+            collective_id=0, has_side_effects=True, vmem_limit_bytes=VMEM_BYTES
+        ),
+    )(x, wanted, bias[:, None, :], embedded[:, :, None], conv_one[0].T, conv_two[0].T, same)
+    one = total[:CH, : 9 * CH].T
+    two = total[CH:, : 9 * CH].T
+    tail = total[:, 9 * CH : 9 * CH + CH // 2]
+    d_time = jnp.concatenate([tail[:TE], tail[TE:]], axis=1)
+    return (one[None], two[None], d_time[None])
+
+
 def solution(mesh):
     placed = (
         P("dp", None, None),
@@ -264,8 +599,10 @@
         P("section", None, None),
         P("section", None, None),
     )
+    two = mesh.shape["section"] == 2 and mesh.shape["dp"] == CORES * CHIPS
+    body = local_two if two else local
     return jax.shard_map(
-        local,
+        body,
         mesh=mesh,
         in_specs=placed,
         out_specs=(P("section", None, None), P("section", None, None), P("section", None, None)),

time: 746 us -> 158 us (0.21)
  local copies, waits for them, and re-layouts: 211 us -> 13.8 us
  waiting for transfers between devices: 186 us -> 0 us
  starting transfers between devices: 159 us -> 0 us
  Pallas kernels: 0 us -> 140 us
  other arithmetic: 122 us -> 2.75 us
  matrix products: 39.7 us -> 0.37 us
  between operations: 14.1 us -> 0.66 us
  loops' own time: 9.1 us -> 0 us
    psum x1 -> x0, waiting for transfers between devices: 171 us -> none  [local(): lax.psum((total_one, total_two, total_time), 'dp')]
    ppermute x12 -> x0, starting transfers between devices: 159 us -> none  [the longest x6 146 us: from_partner(): return lax.ppermute(value, axis, pairs)]
    pallas_call x0 -> x1, Pallas kernels: none -> 140 us  [local_two(): pl.pallas_call(whole_kernel, name='whole', out_shape=jax.ShapeDtypeStruct...]
    scatter-add x28 -> x0, local copies, waits for them, and re-layouts: 105 us -> none  [conv_back(): padded.at[:, row_shift:row_shift + height, col_shift:col_shift + width, :]]
    add x31 -> x0, other arithmetic: 56.5 us -> none  [the longest x3 25.9 us: backward_tick(): total_two + delta_two]
    dot_general x15 -> x1, matrix products: 39.7 us -> 0.37 us  [local_two(): bias = jnp.dot(embedded, time_proj[0], precision=lax.Precision.HIGHEST)]
    concatenate x14 -> x0, local copies, waits for them, and re-layouts: 36.9 us -> none  [patches(): return jnp.concatenate(taps, axis=-1)]
    dynamic_update_slice x12 -> x0, other arithmetic: 17.6 us -> none  [put_slot(): return lax.dynamic_update_index_in_dim(buffer, fresh, slot, 0)]
  transfers between devices with their start and end apart: 13 -> 0, of which waited for: 8 -> 0; matrix products, arithmetic and copies ran while one was open for 7% -> 0% of each run, Pallas kernels for 0% -> 0%
where the time goes in v3:
time: 158 us
  Pallas kernels  140 us (89%)
  local copies, waits for them, and re-layouts  13.8 us (9%)
  other arithmetic  2.75 us (2%)
    pallas_call x1, Pallas kernels, local_two(): pl.pallas_call(whole_kernel, name='whole', out_shape=jax.ShapeDtypeStruct...  140 us
    broadcast_in_dim x1, local copies, waits for them, and re-layouts, local_two(): return (one[None], two[None], d_time[None])  6.82 us

profile of v3, /device:TPU:1, one launch (start us, length us, event | category | flops | bytes accessed | tf_op | source)
XLA Modules:
  0.0 157.5 jit_solution(10845803211266985096)
XLA Ops:
  0.6 0.0 copy-start
  0.7 0.7 convert_element_type.6
  1.4 0.1 multiply_cosine_fusion
  1.5 0.1 fusion.5
  1.6 0.9 copy.9.emb_ref
  2.5 0.0 copy-done
  2.5 0.4 fusion
  2.8 0.6 broadcast_in_dim.19.bias_ref
  3.5 0.9 compare_convert_fusion.same_ref
  4.4 2.1 %reshape.44.x_ref = bf16[2,256,320]{2,1,0:T(8,128)(2,1)} reshape(bf16[2,16,5120]{2,1,0:T(8,128)(2,1)} %param.6) | data formatting | bytes 655360 | tf_op jit(solution)/shard_map/reshape | solution.py:557
  6.4 2.1 %reshape.45.target_ref = bf16[2,256,320]{2,1,0:T(8,128)(2,1)} reshape(bf16[2,16,5120]{2,1,0:T(8,128)(2,1)} %param.7) | data formatting | bytes 655360 | tf_op jit(solution)/shard_map/reshape | solution.py:558
  8.5 139.9 %whole.1 = f32[640,3072]{1,0:T(8,128)} custom-call(bf16[2,256,320]{2,1,0:T(8,128)(2,1)} %reshape.44.x_ref, bf16[2,256,320]{2,1,0:T(8,128)(2,1)} %reshape.45.target_ref, f32[2,1,320]{2,1,0:T(1,128)} %broadcast_in_dim.19.bias_ref, f32[2,320,1]{2,1,0:T(8,128)} %copy.9.emb_ref, bf16[320,2880]{1,0:T(8,128)(2,1)} %bitcast.21, bf16[320,2880]{1,0:T(8,128)(2,1)} %bitcast.22, ...), custom_call_target="tpu_custom_call" | custom-call | tf_op jit(solution)/shard_map/whole/pallas_call | solution.py:565
  148.4 1.3 fusion.7
  149.8 0.9 maximum_bitcast_fusion
  150.7 6.8 %slice_bitcast_fusion = (f32[1,2880,320]{1,2,0:T(8,128)}, f32[1,2880,320]{1,2,0:T(8,128)}) fusion(f32[640,3072]{1,0:T(8,128)} %whole.1), kind=kLoop, calls=%fused_computation | loop fusion | bytes 14745600 | tf_op jit(solution)/shard_map/broadcast_in_dim | solution.py:590
  (2 shorter events, 0.0 us)
Async XLA Ops:
  0.6 1.8 %copy-start = (f32[1,320,320]{2,1,0:T(8,128)S(1)}, f32[1,320,320]{2,1,0:T(8,128)}, u32[]{:S(2)}) copy-start(f32[1,320,320]{2,1,0:T(8,128)} %param.11) | copy-start | bytes 1228804

commit v4 on v3

--- a/solution.py
+++ b/solution.py
@@ -258,9 +258,9 @@
 
 
 PIX = HEIGHT * WIDTH
-KR = 3 * CH
 MESH_IDS = pl.DeviceIdType.MESH
 VMEM_BYTES = 56 * 1024 * 1024
+SUBLANES = 8
 
 
 def group_mean(cols, same_group):
@@ -292,79 +292,56 @@
 
 
 def side_taps(values):
-    column = lax.broadcasted_iota(jnp.int32, (PIX, CH), 0) % WIDTH
-    before = jnp.where(column == 0, 0.0, pltpu.roll(values, 1, 0))
-    after = jnp.where(column == WIDTH - 1, 0.0, pltpu.roll(values, PIX - 1, 0))
+    row = lax.broadcasted_iota(jnp.int32, (PIX, CH), 0) % HEIGHT
+    before = jnp.where(row == 0, 0.0, pltpu.roll(values, 1, 0))
+    after = jnp.where(row == HEIGHT - 1, 0.0, pltpu.roll(values, PIX - 1, 0))
     return before, values, after
 
 
-def add_rows(low, mid, high):
-    edge = jnp.zeros((WIDTH, CH), jnp.float32)
-    down = jnp.concatenate([edge, low[: PIX - WIDTH]], axis=0)
-    up = jnp.concatenate([high[WIDTH:], edge], axis=0)
-    return down + mid + up
+def shifted(values, columns):
+    edge = jnp.zeros((HEIGHT, values.shape[1]), values.dtype)
+    if columns < 0:
+        return jnp.concatenate([edge, values[: PIX - HEIGHT]], axis=0)
+    if columns > 0:
+        return jnp.concatenate([values[HEIGHT:], edge], axis=0)
+    return values
 
 
 def patch_rows(values):
-    taps = jnp.concatenate(side_taps(values), axis=1).astype(jnp.bfloat16)
-    edge = jnp.zeros((WIDTH, KR), jnp.bfloat16)
-    above = jnp.concatenate([edge, taps[: PIX - WIDTH]], axis=0)
-    below = jnp.concatenate([taps[WIDTH:], edge], axis=0)
-    return jnp.concatenate([above, taps, below], axis=1)
+    sides = [side.astype(jnp.bfloat16) for side in side_taps(values)]
+    return jnp.concatenate([shifted(side, c) for side in sides for c in (-1, 0, 1)], axis=1)
 
 
 def conv_rows_back(low, wt_ref):
     spread = jnp.dot(low, wt_ref[...], preferred_element_type=jnp.float32)
-    cols = []
-    for c in range(3):
-        high, mid, down = [
-            spread[:, (3 * r + c) * CH : (3 * r + c + 1) * CH] for r in range(3)
-        ]
-        cols.append(add_rows(down, mid, high))
-    return side_taps(cols[2])[0] + cols[1] + side_taps(cols[0])[2]
-
-
-def weight_rows(patches_low, low, buf_ref, first):
-    buf_ref[first : first + CH, : 9 * CH] += jnp.dot(
-        low.T, patches_low, preferred_element_type=jnp.float32
-    )
-
-
-def taps_of(parts):
+    rows = []
+    for r in range(3):
+        taps = [spread[:, (3 * r + c) * CH : (3 * r + c + 1) * CH] for c in range(3)]
+        rows.append(shifted(taps[2], -1) + taps[1] + shifted(taps[0], 1))
+    return side_taps(rows[2])[0] + rows[1] + side_taps(rows[0])[2]
+
+
+def image_rows(ref, i):
+    lines = ref[i].astype(jnp.float32)
+    return jnp.concatenate([lines[:, w * CH : (w + 1) * CH] for w in range(WIDTH)], axis=0)
+
+
+def activations(parts):
     normed, gate, _ = parts
     return patch_rows(normed * gate)
 
 
-def forward_rows(rows, bias, w1_ref, w2_ref, same_group):
-    parts_a = norm_parts(rows, same_group)
-    taps_a = taps_of(parts_a)
-    mid = jnp.dot(taps_a, w1_ref[...], preferred_element_type=jnp.float32) + bias
-    parts_b = norm_parts(mid, same_group)
-    taps_b = taps_of(parts_b)
-    out = rows + jnp.dot(taps_b, w2_ref[...], preferred_element_type=jnp.float32)
-    return mid, out, parts_a, taps_a, parts_b, taps_b
-
-
-def backward_rows(grad, kept, emb, wt1_ref, wt2_ref, same_group, buf_ref):
-    parts_a, taps_a, parts_b, taps_b = kept
-    low = grad.astype(jnp.bfloat16)
-    back = conv_rows_back(low, wt2_ref)
-    weight_rows(taps_b, low, buf_ref, CH)
-    grad_mid = norm_back(parts_b, back, same_group)
-    d_time = emb * col_sum(grad_mid)
-    half = CH // 2
-    buf_ref[0:TE, 9 * CH : 9 * CH + half] += d_time[:, :half]
-    buf_ref[TE : 2 * TE, 9 * CH : 9 * CH + half] += d_time[:, half:]
-    low = grad_mid.astype(jnp.bfloat16)
-    weight_rows(taps_a, low, buf_ref, 0)
-    back = conv_rows_back(low, wt1_ref)
-    return grad + norm_back(parts_a, back, same_group)
+def group_matrix():
+    assert CH // GROUPS == 10
+    rows = lax.broadcasted_iota(jnp.int32, (CH, CH), 0) * 6554 >> 16
+    cols = lax.broadcasted_iota(jnp.int32, (CH, CH), 1) * 6554 >> 16
+    return jnp.where(rows == cols, 1.0, 0.0)
 
 
 CORES = 2
 CHIPS = 8
 BLOCK = 2 * CH // (CORES * CHIPS)
-SPLITS = ((0, 24), (24, 16))
+SPLITS = tuple((first, 8) for first in range(0, BLOCK, 8))
 SUBS = len(SPLITS)
 LANES = 3072
 
@@ -388,11 +365,14 @@
     return core, place, way, after, before, sibling
 
 
-def meet(others):
+def greet(others):
     barrier = pltpu.get_barrier_semaphore()
     for other in others:
         pl.semaphore_signal(barrier, inc=1, device_id=other, device_id_type=MESH_IDS)
-    pl.semaphore_wait(barrier, len(others))
+
+
+def await_greetings(count):
+    pl.semaphore_wait(pltpu.get_barrier_semaphore(), count)
 
 
 def ring_sum(places, in_ref, out_ref, pair_ref, slot_ref, work_ref, pair_sems, step_sems, turn_sems, give_sems):
@@ -490,16 +470,25 @@
 
 
 def whole_kernel(
-    x_ref, target_ref, bias_ref, emb_ref, wt1_ref, wt2_ref, same_ref,
-    out_ref, w1_ref, w2_ref, mid_ref, send_ref, inbox_ref, buf_ref, send_sems, recv_sems, *ring_refs
+    x_ref, target_ref, emb_ref, proj_ref, wt1_ref, wt2_ref,
+    out_ref, same_ref, bias_ref, dbias_ref, w1_ref, w2_ref, taps1_ref, taps2_ref, low1_ref, low2_ref,
+    mid_ref, send_ref, inbox_ref, buf_ref, send_sems, recv_sems, *ring_refs
 ):
     section = lax.axis_index("section")
     places = ring_places()
     partner = {"section": 1 - section}
-    meet(places[3:] + (partner,))
+    others = places[3:] + (partner,)
+    greet(others)
     images = x_ref.shape[0]
+    highest = lax.Precision.HIGHEST
+    same_ref[...] = group_matrix()
+    bias_ref[...] = jnp.dot(
+        emb_ref[...], proj_ref[0], precision=highest, preferred_element_type=jnp.float32
+    )
+    dbias_ref[...] = jnp.zeros_like(dbias_ref)
     w1_ref[...] = wt1_ref[...].T
     w2_ref[...] = wt2_ref[...].T
+    await_greetings(len(others))
 
     def sent(i):
         return pltpu.make_async_remote_copy(
@@ -511,66 +500,109 @@
             device_id_type=MESH_IDS,
         )
 
+    def rows_of(i):
+        return pl.ds(pl.multiple_of(i * PIX, PIX), PIX)
+
+    def forward(i, rows, same):
+        parts_a = norm_parts(rows, same)
+        taps = activations(parts_a)
+        taps1_ref[rows_of(i), :] = taps
+        mid = jnp.dot(taps, w1_ref[...], preferred_element_type=jnp.float32)
+        mid = mid + bias_ref[pl.ds(i, 1), :]
+        parts_b = norm_parts(mid, same)
+        taps = activations(parts_b)
+        taps2_ref[rows_of(i), :] = taps
+        out = rows + jnp.dot(taps, w2_ref[...], preferred_element_type=jnp.float32)
+        return mid, out, parts_a, parts_b
+
+    def backward_to_mid(i, grad, parts_b, same):
+        low = grad.astype(jnp.bfloat16)
+        low2_ref[rows_of(i), :] = low
+        grad_mid = norm_back(parts_b, conv_rows_back(low, wt2_ref), same)
+        dbias_ref[pl.ds(i, 1), :] = col_sum(grad_mid)
+        low = grad_mid.astype(jnp.bfloat16)
+        low1_ref[rows_of(i), :] = low
+        return low
+
     @pl.when(section == 0)
     def _():
         @pl.loop(0, images)
         def _(i):
-            rows = x_ref[i].astype(jnp.float32)
-            mid, out, *_ = forward_rows(rows, bias_ref[i], w1_ref, w2_ref, same_ref[...])
+            mid, out, *_ = forward(i, image_rows(x_ref, i), same_ref[...])
             mid_ref[i] = mid
             send_ref[i] = out
             sent(i).start()
 
-    buf_ref[...] = jnp.zeros(buf_ref.shape, jnp.float32)
-
-    @pl.when(section == 0)
-    def _():
         @pl.loop(0, images)
         def _(i):
             same = same_ref[...]
-            parts_a = norm_parts(x_ref[i].astype(jnp.float32), same)
             parts_b = norm_parts(mid_ref[i], same)
-            kept = (parts_a, taps_of(parts_a), parts_b, taps_of(parts_b))
             sent(i).wait_recv()
-            grad = inbox_ref[i] + inbox_ref[i]
-            backward_rows(grad, kept, emb_ref[i], wt1_ref, wt2_ref, same, buf_ref)
+            backward_to_mid(i, inbox_ref[i] + inbox_ref[i], parts_b, same)
 
     @pl.when(section == 1)
     def _():
         @pl.loop(0, images)
         def _(i):
             same = same_ref[...]
+            wanted = image_rows(target_ref, i)
             sent(i).wait_recv()
-            rows = inbox_ref[i] + inbox_ref[i]
-            _, out, *kept = forward_rows(rows, bias_ref[i], w1_ref, w2_ref, same)
-            grad = (out - target_ref[i].astype(jnp.float32)) * (1.0 / math.sqrt(PIX))
-            send_ref[i] = backward_rows(grad, kept, emb_ref[i], wt1_ref, wt2_ref, same, buf_ref)
+            _, out, parts_a, parts_b = forward(i, inbox_ref[i] + inbox_ref[i], same)
+            grad = (out - wanted) * (1.0 / math.sqrt(PIX))
+            low = backward_to_mid(i, grad, parts_b, same)
+            send_ref[i] = grad + norm_back(parts_a, conv_rows_back(low, wt1_ref), same)
             sent(i).start()
 
+    for first, low_ref, taps_ref in ((CH, low2_ref, taps2_ref), (0, low1_ref, taps1_ref)):
+        buf_ref[first : first + CH, : 9 * CH] = jnp.dot(
+            low_ref[...].T, taps_ref[...], preferred_element_type=jnp.float32
+        )
+    d_time = jnp.dot(
+        emb_ref[...].T, dbias_ref[...], precision=highest, preferred_element_type=jnp.float32
+    )
+    half = CH // 2
+    blank = jnp.zeros((TE, LANES - 9 * CH - half), jnp.float32)
+    buf_ref[:TE, 9 * CH :] = jnp.concatenate([d_time[:, :half], blank], axis=1)
+    buf_ref[TE:, 9 * CH :] = jnp.concatenate([d_time[:, half:], blank], axis=1)
     for i in range(images):
         sent(i).wait_send()
     ring_sum(places, buf_ref, out_ref, *ring_refs)
 
 
+def unpack_kernel(one_in, two_in, one_ref, two_ref, time_ref):
+    half = CH // 2
+    one_ref[...] = one_in[:, : 9 * CH]
+    two_ref[...] = two_in[:, : 9 * CH]
+    time_ref[...] = jnp.concatenate(
+        [one_in[:, 9 * CH : 9 * CH + half], two_in[:, 9 * CH : 9 * CH + half]], axis=1
+    )
+
+
 def local_two(features, target, timesteps, conv_one, conv_two, time_proj):
     images = features.shape[0]
-    x = features.reshape(images, PIX, CH)
-    wanted = target.reshape(images, PIX, CH)
-    embedded = embed_times(timesteps)
-    bias = jnp.dot(embedded, time_proj[0], precision=lax.Precision.HIGHEST)
-    group = jnp.arange(CH) // (CH // GROUPS)
-    same = (group[:, None] == group[None, :]).astype(jnp.float32)
+    emb_rows = -(-images // SUBLANES) * SUBLANES
+    embedded = embed_times(jnp.pad(timesteps, (0, emb_rows - images)))
     stack = pltpu.VMEM((images, PIX, CH), jnp.float32)
     weight = pltpu.VMEM((9 * CH, CH), jnp.bfloat16)
+    taps = pltpu.VMEM((images * PIX, 9 * CH), jnp.bfloat16)
+    low = pltpu.VMEM((images * PIX, CH), jnp.bfloat16)
+    row = pltpu.VMEM((emb_rows, CH), jnp.float32)
     total = pl.pallas_call(
         whole_kernel,
         name="whole",
         out_shape=jax.ShapeDtypeStruct((2 * CH, LANES), jnp.float32),
-        in_specs=[pl.BlockSpec(memory_space=pltpu.VMEM)] * 7,
+        in_specs=[pl.BlockSpec(memory_space=pltpu.VMEM)] * 6,
         out_specs=pl.BlockSpec(memory_space=pltpu.VMEM),
         scratch_shapes=[
+            pltpu.VMEM((CH, CH), jnp.float32),
+            row,
+            row,
             weight,
             weight,
+            taps,
+            taps,
+            low,
+            low,
             stack,
             stack,
             stack,
@@ -582,12 +614,26 @@
         compiler_params=pltpu.CompilerParams(
             collective_id=0, has_side_effects=True, vmem_limit_bytes=VMEM_BYTES
         ),
-    )(x, wanted, bias[:, None, :], embedded[:, :, None], conv_one[0].T, conv_two[0].T, same)
-    one = total[:CH, : 9 * CH].T
-    two = total[CH:, : 9 * CH].T
-    tail = total[:, 9 * CH : 9 * CH + CH // 2]
-    d_time = jnp.concatenate([tail[:TE], tail[TE:]], axis=1)
-    return (one[None], two[None], d_time[None])
+    )(features, target, embedded, time_proj, conv_one[0].T, conv_two[0].T)
+    step = 64
+    steps = CH // step
+    grad = jax.ShapeDtypeStruct((CH, 9 * CH), jnp.float32)
+    one, two, d_time = pl.pallas_call(
+        unpack_kernel,
+        name="unpack",
+        grid=(steps,),
+        in_specs=[
+            pl.BlockSpec((step, LANES), lambda i: (i, 0)),
+            pl.BlockSpec((step, LANES), lambda i: (i + steps, 0)),
+        ],
+        out_specs=[
+            pl.BlockSpec((step, 9 * CH), lambda i: (i, 0)),
+            pl.BlockSpec((step, 9 * CH), lambda i: (i, 0)),
+            pl.BlockSpec((step, CH), lambda i: (i, 0)),
+        ],
+        out_shape=[grad, grad, jax.ShapeDtypeStruct((TE, CH), jnp.float32)],
+    )(total, total)
+    return (one.T[None], two.T[None], d_time[None])
 
 
 def solution(mesh):

time: 158 us -> 146 us (0.924)
  local copies, waits for them, and re-layouts: 13.8 us -> 0 us
  Pallas kernels: 140 us -> 144 us
    broadcast_in_dim x3 -> x0, local copies, waits for them, and re-layouts: 8.34 us -> none  [the longest x1 6.82 us: local_two(): return (one[None], two[None], d_time[None])]
    pallas_call x0 -> x1, Pallas kernels: none -> 7.95 us  [local_two(): pl.pallas_call(unpack_kernel, name='unpack', grid=(steps,), in_specs=[pl....]
    reshape x2 -> x0, local copies, waits for them, and re-layouts: 4.12 us -> none  [the longest x1 2.06 us: local_two(): x = features.reshape(images, PIX, CH)]
    pallas_call x1, Pallas kernels: 140 us -> 136 us  [local_two(): pl.pallas_call(whole_kernel, name='whole', out_shape=jax.ShapeDtypeStruct...]
where the time goes in v4:
time: 146 us
  Pallas kernels  144 us (99%)
  other arithmetic  1.46 us (1%)
    pallas_call x1, Pallas kernels, local_two(): pl.pallas_call(whole_kernel, name='whole', out_shape=jax.ShapeDtypeStruct...  136 us
    pallas_call x1, Pallas kernels, local_two(): pl.pallas_call(unpack_kernel, name='unpack', grid=(steps,), in_specs=[pl....  7.95 us

profile of v4, /device:TPU:1, one launch (start us, length us, event | category | flops | bytes accessed | tf_op | source)
XLA Modules:
  0.0 145.9 jit_solution(9373220702013641151)
XLA Ops:
  0.6 0.7 pad_convert_fusion
  1.3 0.1 multiply_cosine_fusion
  1.4 0.7 pad_maximum_fusion.emb_ref
  2.1 135.8 %whole.1.one_in.two_in = f32[640,3072]{1,0:T(8,128)} custom-call(bf16[2,16,5120]{2,1,0:T(8,128)(2,1)} %x_ref.1, bf16[2,16,5120]{2,1,0:T(8,128)(2,1)} %target_ref.1, f32[8,320]{1,0:T(8,128)} %pad_maximum_fusion.emb_ref, f32[1,320,320]{2,1,0:T(8,128)} %proj_ref.1, bf16[320,2880]{1,0:T(8,128)(2,1)} %bitcast.13, bf16[320,2880]{1,0:T(8,128)(2,1)} %bitcast.14), custom_call_target="tpu_custom_call" | custom-call | tf_op jit(solution)/shard_map/whole/pallas_call | solution.py:590
  137.9 7.9 %unpack.1 = (f32[320,2880]{1,0:T(8,128)}, f32[320,2880]{1,0:T(8,128)}, f32[320,320]{1,0:T(8,128)}) custom-call(f32[640,3072]{1,0:T(8,128)} %whole.1.one_in.two_in, f32[640,3072]{1,0:T(8,128)} %whole.1.one_in.two_in), custom_call_target="tpu_custom_call" | custom-call | tf_op jit(solution)/shard_map/unpack/pallas_call | solution.py:621
  (1 shorter events, 0.0 us)

commit v5 on v4

--- a/solution.py
+++ b/solution.py
@@ -375,7 +375,7 @@
     pl.semaphore_wait(pltpu.get_barrier_semaphore(), count)
 
 
-def ring_sum(places, in_ref, out_ref, pair_ref, slot_ref, work_ref, pair_sems, step_sems, turn_sems, give_sems):
+def ring_sum(places, in_ref, out_ref, pair_ref, slot_ref, work_ref, pair_sems, step_sems, turn_sems, give_sems, keep_sems):
     core, place, way, after, before, sibling = places
 
     def rows_of(half, block, sub):
@@ -433,24 +433,32 @@
                 arrived[step, sub] = copy
                 pending.append(copy)
             else:
-                out_ref[rows_of(core, block, sub), :] = total
+                kept(work_ref, step, sub)[...] = total
 
     turned = {}
     gifts = []
+    stays = []
     for step in range(CHIPS):
         for sub in range(SUBS):
             block = block_at(CHIPS - 1 + step)
             if step:
                 turned[step - 1, sub].wait_recv()
             here = out_ref.at[rows_of(core, block, sub)]
+            held = here if step else kept(work_ref, CHIPS - 1, sub)
+            if step == 0:
+                copy = pltpu.make_async_copy(held, here, keep_sems.at[sub])
+                copy.start()
+                stays.append(copy)
             if step < CHIPS - 1:
-                copy = remote(here, here, turn_sems, (step, sub), after)
+                copy = remote(held, here, turn_sems, (step, sub), after)
                 copy.start()
                 turned[step, sub] = copy
                 pending.append(copy)
-            copy = remote(here, here, give_sems, (step, sub), sibling)
+            copy = remote(held, here, give_sems, (step, sub), sibling)
             copy.start()
             gifts.append(copy)
+    for copy in stays:
+        copy.wait()
     for copy in gifts:
         copy.wait_recv()
     for copy in pending + gifts:
@@ -461,19 +469,24 @@
     return [
         pltpu.VMEM((CHIPS, BLOCK, LANES), jnp.float32),
         pltpu.VMEM((CHIPS - 1, BLOCK, LANES), jnp.float32),
-        pltpu.VMEM((CHIPS - 1, BLOCK, LANES), jnp.float32),
+        pltpu.VMEM((CHIPS, BLOCK, LANES), jnp.float32),
         pltpu.SemaphoreType.DMA((2, CHIPS, SUBS)),
         pltpu.SemaphoreType.DMA((2, CHIPS - 1, SUBS)),
         pltpu.SemaphoreType.DMA((2, CHIPS - 1, SUBS)),
         pltpu.SemaphoreType.DMA((2, CHIPS, SUBS)),
+        pltpu.SemaphoreType.DMA((SUBS,)),
     ]
 
 
 def whole_kernel(
-    x_ref, target_ref, emb_ref, proj_ref, wt1_ref, wt2_ref,
+    x_ref, target_ref, emb_ref, proj_ref, wt1_hbm, wt2_hbm,
     out_ref, same_ref, bias_ref, dbias_ref, w1_ref, w2_ref, taps1_ref, taps2_ref, low1_ref, low2_ref,
-    mid_ref, send_ref, inbox_ref, buf_ref, send_sems, recv_sems, *ring_refs
+    mid_ref, send_ref, inbox_ref, buf_ref, wt1_ref, wt2_ref, load_sems, send_sems, recv_sems, *ring_refs
 ):
+    load_one = pltpu.make_async_copy(wt1_hbm, wt1_ref, load_sems.at[0])
+    load_two = pltpu.make_async_copy(wt2_hbm, wt2_ref, load_sems.at[1])
+    load_one.start()
+    load_two.start()
     section = lax.axis_index("section")
     places = ring_places()
     partner = {"section": 1 - section}
@@ -486,7 +499,9 @@
         emb_ref[...], proj_ref[0], precision=highest, preferred_element_type=jnp.float32
     )
     dbias_ref[...] = jnp.zeros_like(dbias_ref)
+    load_one.wait()
     w1_ref[...] = wt1_ref[...].T
+    load_two.wait()
     w2_ref[...] = wt2_ref[...].T
     await_greetings(len(others))
 
@@ -591,8 +606,9 @@
         whole_kernel,
         name="whole",
         out_shape=jax.ShapeDtypeStruct((2 * CH, LANES), jnp.float32),
-        in_specs=[pl.BlockSpec(memory_space=pltpu.VMEM)] * 6,
-        out_specs=pl.BlockSpec(memory_space=pltpu.VMEM),
+        in_specs=[pl.BlockSpec(memory_space=pltpu.VMEM)] * 4
+        + [pl.BlockSpec(memory_space=pl.ANY)] * 2,
+        out_specs=pl.BlockSpec(memory_space=pl.ANY),
         scratch_shapes=[
             pltpu.VMEM((CH, CH), jnp.float32),
             row,
@@ -607,6 +623,9 @@
             stack,
             stack,
             pltpu.VMEM((2 * CH, LANES), jnp.float32),
+            pltpu.VMEM((CH, 9 * CH), jnp.bfloat16),
+            pltpu.VMEM((CH, 9 * CH), jnp.bfloat16),
+            pltpu.SemaphoreType.DMA((2,)),
             pltpu.SemaphoreType.DMA((images,)),
             pltpu.SemaphoreType.DMA((images,)),
         ]

time: 146 us -> 144 us (0.986)
  Pallas kernels: 144 us -> 142 us
    pallas_call x1, Pallas kernels: 136 us -> 134 us  [local_two(): pl.pallas_call(whole_kernel, name='whole', out_shape=jax.ShapeDtypeStruct...]
where the time goes in v5:
time: 144 us
  Pallas kernels  142 us (99%)
  other arithmetic  1.46 us (1%)
    pallas_call x1, Pallas kernels, local_two(): pl.pallas_call(whole_kernel, name='whole', out_shape=jax.ShapeDtypeStruct...  134 us
    pallas_call x1, Pallas kernels, local_two(): pl.pallas_call(unpack_kernel, name='unpack', grid=(steps,), in_specs=[pl....  7.95 us

profile of v5, /device:TPU:1, one launch (start us, length us, event | category | flops | bytes accessed | tf_op | source)
XLA Modules:
  0.0 143.9 jit_solution(8913241018447573181)
XLA Ops:
  0.6 0.7 pad_convert_fusion
  1.3 0.1 multiply_cosine_fusion
  1.4 0.7 pad_maximum_fusion.emb_ref
  2.1 133.8 %whole.1.one_in.two_in = f32[640,3072]{1,0:T(8,128)} custom-call(bf16[2,16,5120]{2,1,0:T(8,128)(2,1)} %x_ref.1, bf16[2,16,5120]{2,1,0:T(8,128)(2,1)} %target_ref.1, f32[8,320]{1,0:T(8,128)} %pad_maximum_fusion.emb_ref, f32[1,320,320]{2,1,0:T(8,128)} %proj_ref.1, bf16[320,2880]{1,0:T(8,128)(2,1)} %bitcast.13, bf16[320,2880]{1,0:T(8,128)(2,1)} %bitcast.14), custom_call_target="tpu_custom_call" | custom-call | tf_op jit(solution)/shard_map/whole/pallas_call | solution.py:605
  136.0 7.9 %unpack.1 = (f32[320,2880]{1,0:T(8,128)}, f32[320,2880]{1,0:T(8,128)}, f32[320,320]{1,0:T(8,128)}) custom-call(f32[640,3072]{1,0:T(8,128)} %whole.1.one_in.two_in, f32[640,3072]{1,0:T(8,128)} %whole.1.one_in.two_in), custom_call_target="tpu_custom_call" | custom-call | tf_op jit(solution)/shard_map/unpack/pallas_call | solution.py:640
  (1 shorter events, 0.0 us)
